TPU v7x, 256 devices: a whole 4x4x8 slice. The times are simulated.
256 devices in a mesh: half: 2 (over core), seq: 8 (over z), exp: 16 (over y, x).
Axes of the slice: x: 4, y: 4, z: 8, core: 2. Of those that a mesh axis runs over, the one named last changes fastest.
Arguments:
- prompt_hidden: bfloat16 [2, 8, 16, 256, 5120], P('half', 'seq', 'exp'), may hold values from -6 to 6
- decode_hidden: bfloat16 [2, 8, 16, 4, 5120], P('half', 'seq', 'exp'), may hold values from -6 to 6
- norm_gain: float32 [5120], replicated, may hold values from 0.1 to 1.9
- w_dkv: bfloat16 [5120, 576], replicated, may hold values from -0.078125 to 0.078125
- kv_gain: float32 [512], replicated, may hold values from 0.1 to 1.9
- w_gate: bfloat16 [16, 5120, 1536], P('exp', None, 'seq'), may hold values from -0.078125 to 0.078125
- w_up: bfloat16 [16, 5120, 1536], P('exp', None, 'seq'), may hold values from -0.078125 to 0.078125
- w_down: bfloat16 [16, 1536, 5120], P('exp', 'seq'), may hold values from -0.15625 to 0.15625
- expert_ids: int32 [2, 8, 16, 4, 6], P('half', 'seq', 'exp'), may hold values from 0 to 15, all different within a row; in each aligned block of 4 rows (0 to 3, 4 to 7, ..., all dimensions but the last counted through in order) at most 2 rows name the same one
- gate_values: float32 [2, 8, 16, 4, 6], P('half', 'seq', 'exp'), may hold values from 0.05 to 0.6
- owner: int32 [16, 16], replicated, may hold values from 0 to 15, each once within a row
- prompt_lengths: int32 [256], replicated, may hold values from 64 to 256
- context_lengths: int32 [2, 8, 16, 2], P('half', 'seq', 'exp'), may hold values from 1 to 4095
Outputs:
- moe_out: bfloat16 [2, 8, 16, 4, 5120], P('half', 'seq', 'exp')
- new_latents: bfloat16 [2, 8, 16, 4, 576], P('half', 'seq', 'exp')
- owner_cache: bfloat16 [2, 8, 16, 256, 576], P('half', 'seq', 'exp')
Inputs may be any that keep to these rules, and one draw needn't show every extreme that they name: `expert_ids`: in the 4 rows of one device no expert is named more than 2 times, a bound that some block reaches. Each row is a permutation: every owner takes exactly one prompt of each b.
All inputs are finite; a program needn't handle non-finite values.
Results may differ from a plain program's by a relative error of at most 0.017.
Values may be sent and summed in bfloat16 or wider, within the bound.
A program may use at most 128 MiB of HBM per device.

v0:
```python
import jax
import jax.numpy as jnp
from jax import lax
from jax.sharding import PartitionSpec as P

SPAN = 1


def rms_scale(values, gain):
    mean_sq = jnp.mean(values * values, axis=-1, keepdims=True)
    return values * lax.rsqrt(mean_sq + 1e-06) * gain


def rotate_rope(values, positions):
    halfway = values.shape[-1] // 2
    freq = 10000.0 ** (-(jnp.arange(halfway).astype(jnp.float32) * 2.0 / values.shape[-1]))
    angle = positions.astype(jnp.float32)[..., None] * freq
    first = values[..., :halfway]
    second = values[..., halfway:]
    cosine = jnp.cos(angle)
    sine = jnp.sin(angle)
    return jnp.concatenate(
        [first * cosine - second * sine, second * cosine + first * sine], axis=-1
    )


def make_latents(comp, positions, kv_gain):
    lat_width = kv_gain.shape[0]
    latent = rms_scale(comp[:, :lat_width], kv_gain)
    rotated = rotate_rope(comp[:, lat_width:], positions)
    return jnp.concatenate([latent, rotated], axis=-1).astype(jnp.bfloat16)


def expert_part(rows, w_gate, w_up, w_down):
    gate = jnp.einsum("lnd,ldf->lnf", rows, w_gate, preferred_element_type=jnp.float32)
    upper = jnp.einsum("lnd,ldf->lnf", rows, w_up, preferred_element_type=jnp.float32)
    act = (jax.nn.silu(gate) * upper).astype(jnp.bfloat16)
    return jnp.einsum("lnf,lfd->lnd", act, w_down, preferred_element_type=jnp.float32).astype(
        jnp.bfloat16
    )


def shards(
    prompt_hidden,
    decode_hidden,
    norm_gain,
    w_dkv,
    kv_gain,
    w_gate,
    w_up,
    w_down,
    expert_ids,
    gate_values,
    owner,
    prompt_lengths,
    context_lengths,
):
    rows_n = prompt_hidden.shape[3]
    drows = decode_hidden.shape[3]
    width = prompt_hidden.shape[4]
    top_n = expert_ids.shape[4]
    local_n = w_gate.shape[0]
    seq_n = lax.axis_size("seq")
    exp_n = lax.axis_size("exp")
    experts_n = local_n * exp_n
    cap = drows // 2
    half_idx = lax.axis_index("half")
    seq_idx = lax.axis_index("seq")
    exp_idx = lax.axis_index("exp")
    groups_n = lax.axis_size("half") * seq_n
    pgroups = exp_n // SPAN
    group = half_idx * seq_n + seq_idx
    block = exp_idx // SPAN
    prompt = prompt_hidden.reshape(rows_n, width)
    pnormed = rms_scale(prompt.astype(jnp.float32), norm_gain).astype(jnp.bfloat16)
    pcomp = jnp.dot(pnormed, w_dkv, preferred_element_type=jnp.float32)
    row_ids = jnp.arange(rows_n)
    ppos = exp_idx % SPAN * rows_n + row_ids
    platents = make_latents(pcomp, ppos, kv_gain)
    length = lax.dynamic_index_in_dim(prompt_lengths, group * pgroups + block, 0, keepdims=False)
    keep = ppos < length
    masked = jnp.where(keep[:, None], platents, jnp.zeros_like(platents))
    row_owner = lax.dynamic_index_in_dim(owner, block, 0, keepdims=False)
    group_ids = jnp.arange(groups_n)
    every = lax.all_gather(masked[None], ("half", "seq"), axis=0, tiled=True)
    source = jnp.sum(jnp.where(row_owner == group, group_ids, 0))
    cache = lax.dynamic_index_in_dim(every, source, 0, keepdims=False)
    decode = decode_hidden.reshape(drows, width)
    dnormed = rms_scale(decode.astype(jnp.float32), norm_gain).astype(jnp.bfloat16)
    dcomp = jnp.dot(dnormed, w_dkv, preferred_element_type=jnp.float32)
    drow_ids = jnp.arange(drows)
    dpos = jnp.repeat(context_lengths.reshape(-1), 2) + drow_ids % 2
    new_latents = make_latents(dcomp, dpos, kv_gain)
    flat = expert_ids.reshape(-1)
    onehot = (flat[:, None] == jnp.arange(experts_n)).astype(jnp.int32)
    before = jnp.cumsum(onehot, axis=0) - onehot
    slot = jnp.sum(before * onehot, axis=1)
    place = flat * cap + slot
    source_rows = jnp.repeat(dnormed, top_n, axis=0)
    buffer = jnp.zeros((experts_n * cap, width), jnp.bfloat16).at[place].set(source_rows)
    grouped = buffer.reshape(1, exp_n, local_n, cap, width)
    copies = jnp.broadcast_to(grouped, (seq_n, exp_n, local_n, cap, width)).reshape(
        seq_n * exp_n, local_n, cap, width
    )
    arrived = lax.all_to_all(copies, ("seq", "exp"), split_axis=0, concat_axis=2, tiled=True)
    partial_value = expert_part(arrived[0], w_gate, w_up, w_down)
    returned = lax.all_to_all(
        partial_value[None], ("seq", "exp"), split_axis=2, concat_axis=0, tiled=True
    )
    summed = jnp.sum(returned.reshape(seq_n, experts_n * cap, width).astype(jnp.float32), axis=0)
    expert_out = summed.astype(jnp.bfloat16)
    picked = expert_out[place].reshape(drows, top_n, width).astype(jnp.float32)
    weights = gate_values.reshape(drows, top_n, 1)
    moe_out = jnp.sum(weights * picked, axis=1).astype(jnp.bfloat16)
    return (
        moe_out.reshape(1, 1, 1, drows, width),
        new_latents.reshape(1, 1, 1, drows, -1),
        cache.reshape(1, 1, 1, rows_n, -1),
    )


def solution(mesh):
    in_specs = (
        P("half", "seq", "exp", None, None),
        P("half", "seq", "exp", None, None),
        P(),
        P(),
        P(),
        P("exp", None, "seq"),
        P("exp", None, "seq"),
        P("exp", "seq", None),
        P("half", "seq", "exp", None, None),
        P("half", "seq", "exp", None, None),
        P(),
        P(),
        P("half", "seq", "exp", None),
    )
    out_specs = (
        P("half", "seq", "exp", None, None),
        P("half", "seq", "exp", None, None),
        P("half", "seq", "exp", None, None),
    )
    return jax.shard_map(shards, mesh=mesh, in_specs=in_specs, out_specs=out_specs, check_vma=False)
```

profile of v0, /device:TPU:32, one launch (start us, length us, event | category | flops | bytes accessed | tf_op | source)
XLA Modules:
  0.0 262.4 jit_solution(17108035070081484033)
XLA Ops:
  7.2 0.0 copy-start
  7.2 0.8 broadcast_multiply_fusion
  8.0 0.8 eq.28
  8.8 0.1 mul.192
  8.9 0.1 fusion.44
  9.0 0.2 select_reduce_fusion
  9.2 0.9 fusion.31
  10.1 0.9 fusion.33
  11.0 0.1 reshape.320
  11.1 1.0 scatter_custom_fusion
  12.2 0.1 broadcast_in_dim.30
  12.3 2.9 %broadcast_in_dim.31 = bf16[8,16,2,5120]{3,2,1,0:T(2,128)(2,1)} broadcast(bf16[16,2,5120]{2,1,0:T(2,128)(2,1)S(1)} %broadcast_in_dim.30), dimensions={1,2,3} | broadcast | bytes 2949120 | tf_op jit(solution)/shard_map/broadcast_in_dim | solution.py:102
  15.2 0.0 copy-start.5
  15.2 15.5 %all-to-all-start = ((bf16[128,1,2,5120]{3,2,1,0:T(2,128)(2,1)}), bf16[128,1,2,5120]{3,2,1,0:T(2,128)(2,1)}, u32[]{:S(2)}, u32[]{:S(2)}) async-start(bf16[128,1,2,5120]{3,2,1,0:T(2,128)(2,1)} %bitcast.71), calls=%async_computation | async-start | bytes 5242880 | tf_op jit(solution)/shard_map/all_to_all | solution.py:105
  30.7 0.0 copy-start.2
  30.8 0.0 all-gather.2.cloned.1.call-start
  30.8 0.0 copy-done.5
  30.9 0.0 copy-start.1
  30.9 0.6 dynamic_slice.12
  31.4 0.8 iota_compare_fusion.1
  32.3 2.3 fusion.1
  34.6 0.0 copy-done.2
  34.7 0.0 copy-done.1
  34.7 0.0 copy-start.3
  34.7 4.6 %fusion.4 = f32[256,576]{0,1:T(8,128)S(1)} fusion(bf16[5120,576]{0,1:T(8,128)(2,1)} %param.16, bf16[1,1,1,256,5120]{4,3,2,1,0:T(8,128)(2,1)S(1)} %copy-done.1, f32[5120]{0:T(1024)S(1)} %copy-done.2, f32[256]{0:T(256)S(1)} %add_rsqrt_fusion.1), kind=kOutput, calls=%fused_computation.9 | convolution fusion | flops 1515192320 | bytes 9131008 | tf_op jit(solution)/shard_map/dot_general | solution.py:76
  39.3 0.1 multiply_reduce_fusion.1
  39.4 0.2 fusion.43
  39.6 0.0 copy-done.3
  39.6 0.1 fusion.22
  39.7 0.8 maximum_select_fusion
  40.5 0.0 all-gather.2.cloned.1.call-update
  40.5 70.5 %all-to-all-done = bf16[128,1,2,5120]{3,2,1,0:T(2,128)(2,1)} async-done(((bf16[128,1,2,5120]{3,2,1,0:T(2,128)(2,1)}), bf16[128,1,2,5120]{3,2,1,0:T(2,128)(2,1)}, u32[]{:S(2)}, u32[]{:S(2)}) %all-to-all-start) | async-done | bytes 2621472 | tf_op jit(solution)/shard_map/all_to_all | solution.py:105
  111.0 6.5 %reshape.297 = bf16[256,5120]{1,0:T(8,128)(2,1)} reshape(bf16[128,1,2,5120]{3,2,1,0:T(2,128)(2,1)} %all-to-all-done) | data formatting | bytes 5242880 | tf_op jit(solution)/shard_map/reshape.4
  117.6 3.4 %fusion.12 = f32[256,192]{0,1:T(8,128)S(1)} fusion(bf16[256,5120]{1,0:T(8,128)(2,1)} %reshape.297, bf16[1,5120,192]{1,2,0:T(8,128)(2,1)} %param.18), kind=kOutput, calls=%fused_computation.16 | convolution fusion | flops 503316480 | bytes 4784128 | tf_op jit(solution)/shard_map/lnd,ldf->lnf/dot_general | solution.py:35
  120.9 0.0 copy-done
  120.9 6.9 %fusion = bf16[1,1,256,5120]{3,2,1,0:T(8,128)(2,1)} fusion(bf16[1,192,5120]{2,1,0:T(8,128)(2,1)S(1)} %copy-done, bf16[256,5120]{1,0:T(8,128)(2,1)} %reshape.297, bf16[1,5120,192]{1,2,0:T(8,128)(2,1)} %param.19, f32[256,192]{0,1:T(8,128)S(1)} %fusion.12), kind=kOutput, calls=%fused_computation.5 | convolution fusion | flops 1008238592 | bytes 9371648 | tf_op jit(solution)/shard_map/lnf,lfd->lnd/dot_general | solution.py:38
  127.8 8.1 %copy.20 = bf16[1,1,256,5120]{3,1,0,2:T(2,128)(2,1)} copy(bf16[1,1,256,5120]{3,2,1,0:T(8,128)(2,1)} %fusion) | data formatting | bytes 5242880 | tf_op jit(solution)/shard_map/broadcast_in_dim | solution.py:108
  135.9 0.5 broadcast.193
  136.4 17.0 %reduce.1 = bf16[256,5120]{1,0:T(8,128)(2,1)} reduce(bf16[256,1,1,5120]{3,2,1,0:T(2,128)(2,1)} %bitcast.69, bf16[]{:T(256)} %broadcast.193), dimensions={1,2}, to_apply=%bitcast.68.reduce_sub_computation | reduce | bytes 5242882
  153.4 6.3 %reshape.326 = bf16[128,2,5120]{2,1,0:T(2,128)(2,1)} reshape(bf16[256,5120]{1,0:T(8,128)(2,1)} %reduce.1) | data formatting | bytes 5242880
  159.7 0.0 copy-start.6
  159.7 8.4 %all-to-all-start.1 = ((bf16[128,2,5120]{2,1,0:T(2,128)(2,1)}), bf16[128,2,5120]{2,1,0:T(2,128)(2,1)}, u32[]{:S(2)}, u32[]{:S(2)}) async-start(bf16[128,2,5120]{2,1,0:T(2,128)(2,1)} %reshape.326), calls=%async_computation.1 | async-start | bytes 5242880 | tf_op jit(solution)/shard_map/all_to_all | solution.py:107
  168.1 1.3 fusion.57
  170.7 0.0 copy-done.6
  170.7 0.1 broadcast_in_dim.59
  170.8 0.1 reshape.303
  171.5 4.3 %fusion.61 = f32[4,576]{1,0:T(4,128)S(1)} fusion(bf16[4,5120]{1,0:T(4,128)(2,1)S(1)} %fusion.33, bf16[5120,576]{0,1:T(8,128)(2,1)} %param.16), kind=kOutput, calls=%fused_computation.90 | convolution fusion | flops 23592960 | bytes 5948416 | tf_op jit(solution)/shard_map/dot_general | solution.py:90
  175.8 0.1 multiply_reduce_fusion.2
  176.0 0.1 fusion.55
  176.1 0.1 fusion.45
  176.2 0.7 pad_maximum_fusion
  176.9 0.0 all-gather.2.cloned.1.call-done
  176.9 1.7 dynamic-slice_bitcast_fusion
  178.5 52.0 %all-to-all-done.1 = bf16[128,2,5120]{2,1,0:T(2,128)(2,1)} async-done(((bf16[128,2,5120]{2,1,0:T(2,128)(2,1)}), bf16[128,2,5120]{2,1,0:T(2,128)(2,1)}, u32[]{:S(2)}, u32[]{:S(2)}) %all-to-all-start.1) | async-done | bytes 2621472 | tf_op jit(solution)/shard_map/all_to_all | solution.py:107
  230.6 16.3 %reshape.327 = bf16[256,1,1,5120]{3,2,1,0:T(2,128)(2,1)} reshape(bf16[128,2,5120]{2,1,0:T(2,128)(2,1)} %all-to-all-done.1) | data formatting | bytes 5242880
  246.9 4.8 %copy.18 = bf16[1,1,256,5120]{3,2,0,1:T(8,128)(2,1)} copy(bf16[1,1,256,5120]{3,1,0,2:T(2,128)(2,1)} %bitcast.70) | data formatting | bytes 5242880
  251.7 0.0 copy-start.4
  251.7 2.2 reduce_sum.80
  253.9 0.7 gather_fusion
  254.6 0.1 reshape.306
  254.6 0.0 copy-done.4
  254.6 0.9 multiply_reduce_fusion
  (11 shorter events, 0.1 us)
Async XLA Ops:
  7.2 113.7 %copy-start = (bf16[1,192,5120]{2,1,0:T(8,128)(2,1)S(1)}, bf16[1,192,5120]{2,1,0:T(8,128)(2,1)}, u32[]{:S(2)}) copy-start(bf16[1,192,5120]{2,1,0:T(8,128)(2,1)} %param.20) | copy-start | bytes 5898244
  15.2 15.7 %copy-start.5 = (s32[256]{0:T(256)S(1)}, s32[256]{0:T(256)}, u32[]{:S(2)}) copy-start(s32[256]{0:T(256)} %param.24) | copy-start | bytes 3076
  15.2 95.8 %all-to-all-start = ((bf16[128,1,2,5120]{3,2,1,0:T(2,128)(2,1)}), bf16[128,1,2,5120]{3,2,1,0:T(2,128)(2,1)}, u32[]{:S(2)}, u32[]{:S(2)}) async-start(bf16[128,1,2,5120]{3,2,1,0:T(2,128)(2,1)} %bitcast.71), calls=%async_computation | async-start | bytes 5242880 | tf_op jit(solution)/shard_map/all_to_all | solution.py:105
  30.7 3.9 %copy-start.2 = (f32[5120]{0:T(1024)S(1)}, f32[5120]{0:T(1024)}, u32[]{:S(2)}) copy-start(f32[5120]{0:T(1024)} %param.15) | copy-start | bytes 61444
  30.8 146.1 %all-gather.2.cloned.1.call-start = ((), (), s32[]{:S(2)}) async-start(), calls=%async_computation.2 | async-start | bytes 5013504 | tf_op jit(solution)/shard_map/all_gather | solution.py:85
  30.9 3.8 %copy-start.1 = (bf16[1,1,1,256,5120]{4,3,2,1,0:T(8,128)(2,1)S(1)}, bf16[1,1,1,256,5120]{4,3,2,1,0:T(8,128)(2,1)}, u32[]{:S(2)}) copy-start(bf16[1,1,1,256,5120]{4,3,2,1,0:T(8,128)(2,1)} %param.13) | copy-start | bytes 7864324
  34.7 4.9 %copy-start.3 = (f32[512]{0:T(512)S(1)}, f32[512]{0:T(512)}, u32[]{:S(2)}) copy-start(f32[512]{0:T(512)} %param.17) | copy-start | bytes 6148
  159.7 11.0 %copy-start.6 = (s32[1,1,1,2]{3,2,1,0:T(1,128)S(1)}, s32[1,1,1,2]{3,2,1,0:T(1,128)}, u32[]{:S(2)}) copy-start(s32[1,1,1,2]{3,2,1,0:T(1,128)} %param.25) | copy-start | bytes 28
  159.7 70.9 %all-to-all-start.1 = ((bf16[128,2,5120]{2,1,0:T(2,128)(2,1)}), bf16[128,2,5120]{2,1,0:T(2,128)(2,1)}, u32[]{:S(2)}, u32[]{:S(2)}) async-start(bf16[128,2,5120]{2,1,0:T(2,128)(2,1)} %reshape.326), calls=%async_computation.1 | async-start | bytes 5242880 | tf_op jit(solution)/shard_map/all_to_all | solution.py:107
  251.7 3.0 %copy-start.4 = (f32[1,1,1,4,6]{4,3,2,1,0:T(4,128)S(1)}, f32[1,1,1,4,6]{4,3,2,1,0:T(4,128)}, u32[]{:S(2)}) copy-start(f32[1,1,1,4,6]{4,3,2,1,0:T(4,128)} %param.22) | copy-start | bytes 292
Sparse Core Ops, SparseCore 0:
  40.6 72.6 all-gather.1
where the time goes:
time: 264 us; the launch traced here: 262 us
  waiting for transfers between devices  123 us (47%)
  local copies, waits for them, and re-layouts  50.7 us (19%)
  other arithmetic  29.8 us (11%)
  starting transfers between devices  23.9 us (9%)
  matrix products  19.1 us (7%)
  between operations  16.2 us (6%)
    all_to_all x1, waiting for transfers between devices, shards(): lax.all_to_all(copies, ('seq', 'exp'), split_axis=0, concat_axis=2, tiled...  70.5 us
    all_to_all x1, waiting for transfers between devices, shards(): lax.all_to_all(partial_value[None], ('seq', 'exp'), split_axis=2, concat_...  52 us
    unnamed x18, local copies, waits for them, and re-layouts  27.9 us
    unnamed x1, other arithmetic  17 us
    all_to_all x1, starting transfers between devices, shards(): lax.all_to_all(copies, ('seq', 'exp'), split_axis=0, concat_axis=2, tiled...  15.5 us
    all_to_all x1, starting transfers between devices, shards(): lax.all_to_all(partial_value[None], ('seq', 'exp'), split_axis=2, concat_...  8.36 us
    broadcast_in_dim x1, local copies, waits for them, and re-layouts, shards(): partial_value[None]  8.09 us
    dot_general x1, matrix products, expert_part(): jnp.einsum('lnf,lfd->lnd', act, w_down, preferred_element_type=jnp.float32)  6.89 us
  transfers between devices with their start and end apart: 3, of which 2 were waited for; matrix products, arithmetic and copies ran while one was open for 25% of the time, Pallas kernels for 0%

commit v1 on v0

v1 whole, which is shorter than its diff:
```python
import functools

import jax
import jax.numpy as jnp
import numpy as np
from jax import lax
from jax.experimental import pallas as pl
from jax.experimental.pallas import tpu as pltpu
from jax.sharding import PartitionSpec as P

BF = jnp.bfloat16
F32 = jnp.float32
MESH = pl.DeviceIdType.MESH

D = 5120
LAT = 512
LATW = 576
FB = 192
ROWS = 256
DROWS = 4
TOP = 6
NS = 8
NE = 16
NG = 16
SLOTS = 256
DC = 4
DW = D // DC
META = 128
RC = 5
RW = D // RC
RQ = RW // 4

PLANE = (
    (0, 1), (1, 0), (0, 3), (3, 0), (1, 1), (3, 3), (1, 3), (3, 1),
    (0, 2), (2, 0), (1, 2), (2, 1), (3, 2), (2, 3), (2, 2),
)
ZOFF = (1, 7, 2, 6, 3, 5, 4)
COL = ((1, 0), (0, 1), (0, 7), (1, 1), (1, 7), (0, 2), (0, 6), (1, 2), (1, 6), (0, 3), (0, 5), (1, 3), (1, 5), (0, 4), (1, 4))

NT = (((1,), (1,)), ((), ()))


def iota(shape, dim):
    return lax.broadcasted_iota(jnp.int32, shape, dim)


def wait_bytes(ref, sem):
    pltpu.make_async_copy(ref, ref, sem).wait()


def latents(comp, pos, kv_gain, freq):
    lat = comp[:, :LAT]
    ms = jnp.mean(lat * lat, axis=-1, keepdims=True)
    lat = lat * lax.rsqrt(ms + 1e-06) * kv_gain
    rot = comp[:, LAT:]
    angle = pos * freq
    sine = jnp.sin(angle)
    swapped = jnp.concatenate([rot[:, 32:], rot[:, :32]], axis=-1)
    lane = iota(rot.shape, 1)
    rot = rot * jnp.cos(angle) + jnp.where(lane < 32, -sine, sine) * swapped
    return lat, rot


def kernel(
    dh, ng, kg, freq, ids, gates, owner, plen, ctx, ph_hbm, wk_hbm, wg_hbm, wu_hbm, wd_hbm,
    moe_out, newlat_out, cache_out,
    ph, wk, wgu, wd, xp, comp, msg, gath, sbuf, xbuf, hacc, actb, ybuf, rbuf, fbuf, qbuf, pbuf, abuf, bbuf, cbuf,
    lsem, zs, zr, ds_, dr, p1s, p1r, p2s, p2r, rs, rr, fs, fr,
):
    h = lax.axis_index("half")
    s = lax.axis_index("seq")
    e = lax.axis_index("exp")
    y = e // 4
    x = e % 4
    g = h * NS + s
    plane_ids = [((y + dy) % 4) * 4 + (x + dx) % 4 for dy, dx in PLANE]
    z_ids = [(s + d) % NS for d in ZOFF]
    col_ids = [((h + dh_) % 2, (s + d) % NS) for dh_, d in COL]

    barrier = pltpu.get_barrier_semaphore()
    for p in plane_ids:
        pl.semaphore_signal(barrier, inc=1, device_id=(h, s, p), device_id_type=MESH)
    for hp, sp in col_ids:
        pl.semaphore_signal(barrier, inc=1, device_id=(hp, sp, e), device_id_type=MESH)

    loads = [
        pltpu.make_async_copy(ph_hbm, ph, lsem.at[0]),
        pltpu.make_async_copy(wk_hbm, wk, lsem.at[1]),
        pltpu.make_async_copy(wg_hbm, wgu.at[pl.ds(0, FB)], lsem.at[2]),
        pltpu.make_async_copy(wu_hbm, wgu.at[pl.ds(FB, FB)], lsem.at[3]),
        pltpu.make_async_copy(wd_hbm, wd, lsem.at[4]),
    ]
    for c in loads:
        c.start()

    dec = dh[...].astype(F32)
    ms = jnp.mean(dec * dec, axis=-1, keepdims=True)
    dn = dec * lax.rsqrt(ms + 1e-06) * ng[...]
    msg[:, pl.ds(0, DW)] = jnp.concatenate([dn[:, q * DW:(q + 1) * DW] for q in range(4)], axis=0).astype(BF)
    xp[pl.ds(ROWS, 16), :] = jnp.concatenate([dn, jnp.zeros((12, D), F32)], axis=0).astype(BF)
    lane = iota((1, META), 1)
    kind = lane // 32
    xl = (lane % 32) // 2
    cl = lane % 2
    before = jnp.zeros((1, META), jnp.int32)
    rows = []
    for r in range(DROWS):
        named = jnp.zeros((1, META), jnp.int32)
        gv = jnp.zeros((1, META), F32)
        for k in range(TOP):
            hit = xl == ids[r, k]
            named = named + jnp.where(hit, 1, 0)
            gv = gv + jnp.where(hit, gates[r, k], 0.0)
        hi = gv.astype(BF).astype(F32)
        val = jnp.where(kind == 0, 1.0, jnp.where(kind == 1, hi, jnp.where(kind == 2, gv - hi, 0.0)))
        rows.append(jnp.where((named > 0) & (before == cl), val, 0.0))
        before = before + named
    meta4 = jnp.concatenate(rows, axis=0)
    msg[:, pl.ds(DW, META)] = jnp.concatenate([meta4] * 4, axis=0).astype(BF)

    pl.semaphore_wait(barrier, len(PLANE) + len(COL))

    my_rows = pl.ds(pl.multiple_of(s * 16, 16), 16)
    for p in z_ids:
        pltpu.make_async_remote_copy(msg, gath.at[my_rows], zs, zr, device_id=(h, p, e), device_id_type=MESH).start()
    gath[my_rows, :] = msg[...]

    loads[0].wait()

    def pnorm(i, _):
        at = pl.ds(pl.multiple_of(i * 32, 32), 32)
        v = ph[at, :].astype(F32)
        m = jnp.mean(v * v, axis=-1, keepdims=True)
        xp[at, :] = (v * lax.rsqrt(m + 1e-06) * ng[...]).astype(BF)
        return 0

    lax.fori_loop(0, ROWS // 32, pnorm, 0)

    wait_bytes(gath.at[pl.ds(0, 112)], zr)
    mt = gath[:, pl.ds(DW, META)]
    ei = iota((SLOTS, META), 0)
    ej = iota((SLOTS, META), 1)
    same = ((ei // 16) == ((ej % 32) // 2)) & ((ei % 2) == (ej % 2))
    et_slot = jnp.where(same & (ej // 32 == 0), 1.0, 0.0).astype(BF)
    et_gate = jnp.where(same & ((ej // 32 == 1) | (ej // 32 == 2)), 1.0, 0.0).astype(BF)
    t2 = lax.dot_general(et_slot, mt, NT, preferred_element_type=F32)
    samez = ((ei // 2) % 8) == (ej // 16)
    own = pl.ds(pl.multiple_of(e * 16, 16), 16)

    def dispatch(q, _):
        sel = jnp.where(samez & ((ej // 4) % 4 == q), t2, 0.0).astype(BF)
        sbuf[q] = jnp.dot(sel, gath[:, pl.ds(0, DW)], preferred_element_type=F32).astype(BF)
        for p in plane_ids:
            pltpu.make_async_remote_copy(
                sbuf.at[q, pl.ds(pl.multiple_of(p * 16, 16), 16)], xbuf.at[q, own], ds_.at[q], dr.at[q],
                device_id=(h, s, p), device_id_type=MESH).start()
        xbuf[q, own, :] = sbuf[q, own, :]
        return 0

    lax.fori_loop(0, DC, dispatch, 0)

    loads[1].wait()
    comp[...] = jnp.zeros_like(comp)

    def compress(i, _):
        at = pl.ds(pl.multiple_of(i * 1024, 1024), 1024)
        comp[...] += lax.dot_general(xp[:, at], wk[:, at], NT, preferred_element_type=F32)
        return 0

    lax.fori_loop(0, D // 1024, compress, 0)
    length = plen[g * NE + e]

    def prompt_latents(i, _):
        at = pl.ds(pl.multiple_of(i * 64, 64), 64)
        rid = iota((64, 1), 0) + i * 64
        lat, rot = latents(comp[at, :], rid.astype(F32), kg[...], freq[...])
        pbuf[at, pl.ds(0, LAT)] = jnp.where(rid < length, lat, 0.0).astype(BF)
        pbuf[at, pl.ds(LAT, 64)] = jnp.where(rid < length, rot, 0.0).astype(BF)
        return 0

    lax.fori_loop(0, ROWS // 64, prompt_latents, 0)
    mine = pl.ds(pl.multiple_of(g * 16, 16), 16)
    for hp, sp in col_ids:
        pltpu.make_async_remote_copy(
            pbuf.at[pl.ds(pl.multiple_of((hp * NS + sp) * 16, 16), 16)], abuf.at[mine], p1s, p1r,
            device_id=(hp, sp, e), device_id_type=MESH).start()
    abuf[mine, :] = pbuf[mine, :]

    rid = iota((16, 1), 0)
    dpos = jnp.where(rid < 2, ctx[0, 0], ctx[0, 1]) + rid % 2
    lat, rot = latents(comp[pl.ds(ROWS, 16), :], dpos.astype(F32), kg[...], freq[...])
    newlat_out[:, pl.ds(0, LAT)] = lat[:DROWS].astype(BF)
    newlat_out[:, pl.ds(LAT, 64)] = rot[:DROWS].astype(BF)

    lane = iota((1, ROWS), 1)
    to = jnp.zeros((1, ROWS), jnp.int32)
    for k in range(NG):
        to = to + jnp.where(lane // 16 == k, owner[e, k], 0)
    pi = iota((ROWS, ROWS), 0)
    pj = iota((ROWS, ROWS), 1)
    perm = jnp.where((pi // 16 == to) & (pi % 16 == pj % 16), 1.0, 0.0).astype(BF)
    wait_bytes(abuf.at[pl.ds(0, 240)], p1r)
    bbuf[...] = jnp.dot(perm, abuf[...], preferred_element_type=F32).astype(BF)
    for hp, sp in col_ids:
        pltpu.make_async_remote_copy(
            bbuf.at[pl.ds(pl.multiple_of((hp * NS + sp) * 16, 16), 16)], cbuf.at[mine], p2s, p2r,
            device_id=(hp, sp, e), device_id_type=MESH).start()
    cbuf[mine, :] = bbuf[mine, :]

    loads[2].wait()
    loads[3].wait()
    hacc[...] = jnp.zeros_like(hacc)

    def up(q, _):
        wait_bytes(xbuf.at[q, pl.ds(0, 240)], dr.at[q])
        at = pl.ds(pl.multiple_of(q * DW, DW), DW)
        hacc[...] += lax.dot_general(xbuf[q], wgu[:, at], NT, preferred_element_type=F32)
        return 0

    lax.fori_loop(0, DC, up, 0)
    gate = hacc[:, pl.ds(0, FB)]
    actb[...] = (gate * jax.nn.sigmoid(gate) * hacc[:, pl.ds(FB, FB)]).astype(BF)
    loads[4].wait()

    def down(k, _):
        at = pl.ds(pl.multiple_of(k * RW, RW), RW)
        ybuf[k] = jnp.dot(actb[...], wd[:, at], preferred_element_type=F32).astype(BF)
        for p in plane_ids:
            pltpu.make_async_remote_copy(
                ybuf.at[k, pl.ds(pl.multiple_of(p * 16, 16), 16)], rbuf.at[k, own], rs.at[k], rr.at[k],
                device_id=(h, s, p), device_id_type=MESH).start()
        rbuf[k, own, :] = ybuf[k, own, :]
        return 0

    lax.fori_loop(0, RC, down, 0)

    wait_bytes(cbuf.at[pl.ds(0, 240)], p2r)
    cache_out[...] = cbuf[...].astype(F32).T.astype(BF)

    cg = lax.dot_general(gath[:, pl.ds(DW, META)], et_gate, NT, preferred_element_type=F32)
    ci = iota((META, SLOTS), 0)
    cj = iota((META, SLOTS), 1)
    cz = (ci // 16) == ((cj // 2) % 8)

    def combine(k, _):
        wait_bytes(rbuf.at[k, pl.ds(0, 240)], rr.at[k])
        total = jnp.zeros((META, RQ), F32)
        for q in range(4):
            w = jnp.where(cz & ((ci // 4) % 4 == q), cg, 0.0)
            hi = w.astype(BF)
            lo = (w - hi.astype(F32)).astype(BF)
            part = rbuf[k, :, pl.ds(q * RQ, RQ)]
            total += jnp.dot(hi, part, preferred_element_type=F32)
            total += jnp.dot(lo, part, preferred_element_type=F32)
        fbuf[k] = total.astype(BF)
        for p in z_ids:
            pltpu.make_async_remote_copy(
                fbuf.at[k, pl.ds(pl.multiple_of(p * 16, 16), 16)], qbuf.at[k, my_rows], fs.at[k], fr.at[k],
                device_id=(h, p, e), device_id_type=MESH).start()
        qbuf[k, my_rows, :] = fbuf[k, my_rows, :]
        return 0

    lax.fori_loop(0, RC, combine, 0)

    for k in range(RC):
        wait_bytes(qbuf.at[k, pl.ds(0, 112)], fr.at[k])
        tot = jnp.zeros((16, RQ), F32)
        for z in range(NS):
            tot += qbuf[k, pl.ds(z * 16, 16), :].astype(F32)
        for q in range(4):
            moe_out[:, pl.ds(k * RW + q * RQ, RQ)] = tot[q * 4:q * 4 + 4, :].astype(BF)

    for k in range(RC):
        wait_bytes(fbuf.at[k, pl.ds(0, 112)], fs.at[k])
        wait_bytes(ybuf.at[k, pl.ds(0, 240)], rs.at[k])
    for q in range(DC):
        wait_bytes(sbuf.at[q, pl.ds(0, 240)], ds_.at[q])
    wait_bytes(gath.at[pl.ds(0, 112)], zs)
    wait_bytes(pbuf.at[pl.ds(0, 240)], p1s)
    wait_bytes(bbuf.at[pl.ds(0, 240)], p2s)


def shards(
    prompt_hidden, decode_hidden, norm_gain, w_dkv, kv_gain, w_gate, w_up, w_down, expert_ids, gate_values,
    owner, prompt_lengths, context_lengths,
):
    freq = 10000.0 ** (-(np.arange(32, dtype=np.float64) * 2.0 / 64))
    freq = jnp.asarray(np.concatenate([freq, freq])[None, :], F32)
    vm = pl.BlockSpec(memory_space=pltpu.VMEM)
    sm = pl.BlockSpec(memory_space=pltpu.SMEM)
    hbm = pl.BlockSpec(memory_space=pl.ANY)
    dma = pltpu.SemaphoreType.DMA
    moe, newlat, cache = pl.pallas_call(
        kernel,
        out_shape=(
            jax.ShapeDtypeStruct((DROWS, D), BF),
            jax.ShapeDtypeStruct((DROWS, LATW), BF),
            jax.ShapeDtypeStruct((LATW, ROWS), BF),
        ),
        in_specs=[vm] * 4 + [sm] * 5 + [hbm] * 5,
        out_specs=(vm, vm, vm),
        scratch_shapes=[
            pltpu.VMEM((ROWS, D), BF),
            pltpu.VMEM((LATW, D), BF),
            pltpu.VMEM((2 * FB, D), BF),
            pltpu.VMEM((FB, D), BF),
            pltpu.VMEM((ROWS + 16, D), BF),
            pltpu.VMEM((ROWS + 16, LATW), F32),
            pltpu.VMEM((16, DW + META), BF),
            pltpu.VMEM((NS * 16, DW + META), BF),
            pltpu.VMEM((DC, SLOTS, DW), BF),
            pltpu.VMEM((DC, SLOTS, DW), BF),
            pltpu.VMEM((SLOTS, 2 * FB), F32),
            pltpu.VMEM((SLOTS, FB), BF),
            pltpu.VMEM((RC, SLOTS, RW), BF),
            pltpu.VMEM((RC, SLOTS, RW), BF),
            pltpu.VMEM((RC, NS * 16, RQ), BF),
            pltpu.VMEM((RC, NS * 16, RQ), BF),
            pltpu.VMEM((ROWS, LATW), BF),
            pltpu.VMEM((ROWS, LATW), BF),
            pltpu.VMEM((ROWS, LATW), BF),
            pltpu.VMEM((ROWS, LATW), BF),
            dma((5,)), dma, dma, dma((DC,)), dma((DC,)), dma, dma, dma, dma, dma((RC,)), dma((RC,)), dma((RC,)), dma((RC,)),
        ],
        compiler_params=pltpu.CompilerParams(collective_id=0, has_side_effects=True, vmem_limit_bytes=56 * 2**20),
        cost_estimate=pl.CostEstimate(flops=4 * 10**9, bytes_accessed=16 * 10**6, transcendentals=10**5),
        name="layer_slice",
    )(
        decode_hidden.reshape(DROWS, D), norm_gain.reshape(1, D), kv_gain.reshape(1, LAT), freq,
        expert_ids.reshape(DROWS, TOP), gate_values.reshape(DROWS, TOP), owner, prompt_lengths,
        context_lengths.reshape(1, 2),
        prompt_hidden.reshape(ROWS, D), w_dkv.T, w_gate[0].T, w_up[0].T, w_down[0],
    )
    return (
        moe.reshape(1, 1, 1, DROWS, D),
        newlat.reshape(1, 1, 1, DROWS, LATW),
        cache.T.reshape(1, 1, 1, ROWS, LATW),
    )


def solution(mesh):
    token = P("half", "seq", "exp", None, None)
    in_specs = (
        token, token, P(), P(), P(), P("exp", None, "seq"), P("exp", None, "seq"), P("exp", "seq", None),
        token, token, P(), P(), P("half", "seq", "exp", None),
    )
    return jax.shard_map(shards, mesh=mesh, in_specs=in_specs, out_specs=(token, token, token), check_vma=False)
```

time: 264 us -> 95.7 us (0.36)
  waiting for transfers between devices: 123 us -> 0 us
  Pallas kernels: 0 us -> 90.3 us
  local copies, waits for them, and re-layouts: 50.7 us -> 4.39 us
  other arithmetic: 29.8 us -> 0 us
  starting transfers between devices: 23.9 us -> 0 us
  matrix products: 19.1 us -> 0 us
  between operations: 16.2 us -> 0.64 us
    all_to_all x2 -> x0, waiting for transfers between devices: 123 us -> none  [the longest x1 70.5 us: shards(): lax.all_to_all(copies, ('seq', 'exp'), split_axis=0, concat_axis=2, tiled...]
    pallas_call x0 -> x1, Pallas kernels: none -> 90.3 us  [shards(): pl.pallas_call(kernel, out_shape=(jax.ShapeDtypeStruct((DROWS, D), BF), j...]
    all_to_all x2 -> x0, starting transfers between devices: 23.9 us -> none  [the longest x1 15.5 us: shards(): lax.all_to_all(copies, ('seq', 'exp'), split_axis=0, concat_axis=2, tiled...]
    unnamed x18 -> x3, local copies, waits for them, and re-layouts: 27.9 us -> 4.39 us
    dot_general x4 -> x0, matrix products: 19.1 us -> none  [the longest x1 6.89 us: expert_part(): jnp.einsum('lnf,lfd->lnd', act, w_down, preferred_element_type=jnp.float32)]
    unnamed x1 -> x0, other arithmetic: 17 us -> none
    broadcast_in_dim x5 -> x0, local copies, waits for them, and re-layouts: 11.2 us -> none  [the longest x1 8.09 us: shards(): partial_value[None]]
    reduce_sum x8 -> x0, other arithmetic: 8.07 us -> none  [the longest x4 3.49 us: rms_scale(): mean_sq = jnp.mean(values * values, axis=-1, keepdims=True)]
  transfers between devices with their start and end apart: 3 -> 0, of which waited for: 2 -> 0; matrix products, arithmetic and copies ran while one was open for 25% -> 0% of each run, Pallas kernels for 0% -> 0%
where the time goes in v1:
time: 95.7 us; the launch traced here: 95.4 us
  Pallas kernels  90.3 us (94%)
  local copies, waits for them, and re-layouts  4.39 us (5%)
    pallas_call x1, Pallas kernels, shards(): pl.pallas_call(kernel, out_shape=(jax.ShapeDtypeStruct((DROWS, D), BF), j...  90.3 us
    unnamed x3, local copies, waits for them, and re-layouts  4.39 us

profile of v1, /device:TPU:32, one launch (start us, length us, event | category | flops | bytes accessed | tf_op | source)
XLA Modules:
  0.0 95.4 jit_solution(4694539555054588895)
XLA Ops:
  0.6 90.3 %layer_slice.1 = (bf16[4,5120]{1,0:T(4,128)(2,1)}, bf16[4,576]{1,0:T(4,128)(2,1)}, bf16[576,256]{1,0:T(8,128)(2,1)}) custom-call(bf16[4,5120]{1,0:T(4,128)(2,1)} %bitcast.28, f32[1,5120]{1,0:T(1,128)} %bitcast.29, f32[1,512]{1,0:T(1,128)} %bitcast.30, f32[1,64]{1,0:T(1,128)} %constant.2.clone.freq, s32[4,6]{1,0:T(4,128)} %bitcast.31, f32[4,6]{1,0:T(4,128)} %bitcast.32, ...), custom_call_target="tpu_custom_call" | custom-call | flops 4000000000 | bytes 16000000 | tf_op jit(solution)/shard_map/layer_slice/pallas_call | solution.py:293
  91.0 1.4 %copy.20 = bf16[1,1,1,4,5120]{4,3,2,1,0:T(4,128)(2,1)} copy(bf16[1,1,1,4,5120]{4,3,2,1,0:T(4,128)(2,1)} %bitcast.21) | data formatting | bytes 81920
  92.4 1.3 %copy.21 = bf16[1,1,1,4,576]{4,3,2,1,0:T(4,128)(2,1)} copy(bf16[1,1,1,4,576]{4,3,2,1,0:T(4,128)(2,1)} %bitcast.22) | data formatting | bytes 9216
  93.7 1.7 %copy.22 = bf16[1,1,1,256,576]{3,4,2,1,0:T(8,128)(2,1)} copy(bf16[1,1,1,256,576]{3,4,2,1,0:T(8,128)(2,1)} %bitcast.20) | data formatting | bytes 589824

commit v2 on v1

--- a/solution.py
+++ b/solution.py
@@ -23,18 +23,24 @@
 NE = 16
 NG = 16
 SLOTS = 256
+CZ = 3072
+CP = D - CZ
+HP = CP // 2
 DC = 4
-DW = D // DC
+DW = CZ // DC
+MW = CZ // 8
 META = 128
-RC = 5
-RW = D // RC
+RC = 3
+RW = CZ // RC
 RQ = RW // 4
+PQ = 8
+PW = CP // PQ
 
 PLANE = (
     (0, 1), (1, 0), (0, 3), (3, 0), (1, 1), (3, 3), (1, 3), (3, 1),
     (0, 2), (2, 0), (1, 2), (2, 1), (3, 2), (2, 3), (2, 2),
 )
-ZOFF = (1, 7, 2, 6, 3, 5, 4)
+ZOFF = (4, 3, 5, 2, 6, 1, 7)
 COL = ((1, 0), (0, 1), (0, 7), (1, 1), (1, 7), (0, 2), (0, 6), (1, 2), (1, 6), (0, 3), (0, 5), (1, 3), (1, 5), (0, 4), (1, 4))
 
 NT = (((1,), (1,)), ((), ()))
@@ -65,7 +71,9 @@
     dh, ng, kg, freq, ids, gates, owner, plen, ctx, ph_hbm, wk_hbm, wg_hbm, wu_hbm, wd_hbm,
     moe_out, newlat_out, cache_out,
     ph, wk, wgu, wd, xp, comp, msg, gath, sbuf, xbuf, hacc, actb, ybuf, rbuf, fbuf, qbuf, pbuf, abuf, bbuf, cbuf,
+    mtp, pmsg, parr, pxb, ypb, sumr, suml, gotr, gotl, pfold, pback, wts,
     lsem, zs, zr, ds_, dr, p1s, p1r, p2s, p2r, rs, rr, fs, fr,
+    ps, pr, gs, gr, us, ur, bs, br,
 ):
     h = lax.axis_index("half")
     s = lax.axis_index("seq")
@@ -96,7 +104,9 @@
     dec = dh[...].astype(F32)
     ms = jnp.mean(dec * dec, axis=-1, keepdims=True)
     dn = dec * lax.rsqrt(ms + 1e-06) * ng[...]
-    msg[:, pl.ds(0, DW)] = jnp.concatenate([dn[:, q * DW:(q + 1) * DW] for q in range(4)], axis=0).astype(BF)
+    for i, at in enumerate((0, MW + META)):
+        msg[:, pl.ds(at, MW)] = jnp.concatenate(
+            [dn[:, (4 * i + q) * MW:(4 * i + q + 1) * MW] for q in range(4)], axis=0).astype(BF)
     xp[pl.ds(ROWS, 16), :] = jnp.concatenate([dn, jnp.zeros((12, D), F32)], axis=0).astype(BF)
     lane = iota((1, META), 1)
     kind = lane // 32
@@ -116,14 +126,33 @@
         rows.append(jnp.where((named > 0) & (before == cl), val, 0.0))
         before = before + named
     meta4 = jnp.concatenate(rows, axis=0)
-    msg[:, pl.ds(DW, META)] = jnp.concatenate([meta4] * 4, axis=0).astype(BF)
+    msg[:, pl.ds(MW, META)] = jnp.concatenate([meta4] * 4, axis=0).astype(BF)
+
+    mtp[...] = jnp.concatenate([meta4] * PQ, axis=0).astype(BF)
+    fi = iota((SLOTS, META), 0)
+    fj = iota((SLOTS, META), 1)
+    fsame = ((fi // 16) == ((fj % 32) // 2)) & (((fi // 8) % 2) == (fj % 2))
+    fold_slot = jnp.where(fsame & (fj // 32 == 0), 1.0, 0.0).astype(BF)
+    tf = lax.dot_general(fold_slot, mtp[...], NT, preferred_element_type=F32)
+    self_ = jnp.where(iota((SLOTS, 4 * PQ), 0) % PQ == iota((SLOTS, 4 * PQ), 1) // 4, tf, 0.0).astype(BF)
+    dcols = jnp.concatenate([dn[:, CZ + q * PW:CZ + (q + 1) * PW] for q in range(PQ)], axis=0).astype(BF)
+    pmsg[...] = jnp.dot(self_, dcols, preferred_element_type=F32).astype(BF)
 
     pl.semaphore_wait(barrier, len(PLANE) + len(COL))
 
     my_rows = pl.ds(pl.multiple_of(s * 16, 16), 16)
-    for p in z_ids:
-        pltpu.make_async_remote_copy(msg, gath.at[my_rows], zs, zr, device_id=(h, p, e), device_id_type=MESH).start()
+    own = pl.ds(pl.multiple_of(e * 16, 16), 16)
+    pieces = (pl.ds(0, MW + META), pl.ds(MW + META, MW))
+    for i, cols in enumerate(pieces):
+        for p in z_ids:
+            pltpu.make_async_remote_copy(
+                msg.at[:, cols], gath.at[my_rows, cols], zs.at[i], zr.at[i], device_id=(h, p, e), device_id_type=MESH).start()
+    for p in plane_ids:
+        pltpu.make_async_remote_copy(
+            pmsg.at[pl.ds(pl.multiple_of(p * 16, 16), 16)], parr.at[own], ps, pr,
+            device_id=(h, s, p), device_id_type=MESH).start()
     gath[my_rows, :] = msg[...]
+    parr[own, :] = pmsg[own, :]
 
     loads[0].wait()
 
@@ -136,8 +165,73 @@
 
     lax.fori_loop(0, ROWS // 32, pnorm, 0)
 
-    wait_bytes(gath.at[pl.ds(0, 112)], zr)
-    mt = gath[:, pl.ds(DW, META)]
+    right = (s + 1) % NS
+    left = (s + 7) % NS
+
+    sides = (right, left)
+    halves = (pl.ds(0, HP), pl.ds(HP, HP))
+
+    def block(d, t):
+        return (s + NS - t) % NS if d == 0 else (s + t) % NS
+
+    def gather_send(d, t, u):
+        if t > 0:
+            wait_bytes(pxb.at[block(d, t), :, halves[u]], gr.at[d, t - 1, u])
+        part = pxb.at[block(d, t), :, halves[u]]
+        pltpu.make_async_remote_copy(
+            part, part, gs.at[d, t, u], gr.at[d, t, u], device_id=(h, sides[d], e), device_id_type=MESH).start()
+
+    def gather_step(t):
+        for d in range(2):
+            gather_send(d, t, d)
+        if t < 3:
+            for d in range(2):
+                gather_send(d, t, 1 - d)
+
+    def gather_end():
+        for d in range(2):
+            wait_bytes(pxb.at[block(d, 4), :, halves[d]], gr.at[d, 3, d])
+            wait_bytes(pxb.at[block(d, 3), :, halves[1 - d]], gr.at[d, 2, 1 - d])
+
+    ui = iota((SLOTS, SLOTS), 0)
+    uj = iota((SLOTS, SLOTS), 1)
+    unfold = jnp.where(uj == ((ui % 32) // 2) * 16 + (ui % 2) * 8 + ui // 32, 1.0, 0.0).astype(BF)
+    wait_bytes(parr.at[pl.ds(0, 240)], pr)
+    flat = jnp.dot(unfold, parr[...], preferred_element_type=F32).astype(BF)
+    for q in range(PQ):
+        pxb[s, :, pl.ds(q * PW, PW)] = flat[q * 32:(q + 1) * 32, :]
+    gather_step(0)
+
+    loads[1].wait()
+    comp[...] = jnp.zeros_like(comp)
+
+    def compress(i, _):
+        at = pl.ds(pl.multiple_of(i * 1024, 1024), 1024)
+        comp[...] += lax.dot_general(xp[:, at], wk[:, at], NT, preferred_element_type=F32)
+        return 0
+
+    lax.fori_loop(0, D // 1024, compress, 0)
+    length = plen[g * NE + e]
+
+    def prompt_latents(i, _):
+        at = pl.ds(pl.multiple_of(i * 64, 64), 64)
+        rid = iota((64, 1), 0) + i * 64
+        lat, rot = latents(comp[at, :], rid.astype(F32), kg[...], freq[...])
+        pbuf[at, pl.ds(0, LAT)] = jnp.where(rid < length, lat, 0.0).astype(BF)
+        pbuf[at, pl.ds(LAT, 64)] = jnp.where(rid < length, rot, 0.0).astype(BF)
+        return 0
+
+    lax.fori_loop(0, ROWS // 64, prompt_latents, 0)
+    mine = pl.ds(pl.multiple_of(g * 16, 16), 16)
+    for hp, sp in col_ids:
+        pltpu.make_async_remote_copy(
+            pbuf.at[pl.ds(pl.multiple_of((hp * NS + sp) * 16, 16), 16)], abuf.at[mine], p1s, p1r,
+            device_id=(hp, sp, e), device_id_type=MESH).start()
+    abuf[mine, :] = pbuf[mine, :]
+
+
+    wait_bytes(gath.at[pl.ds(0, 112), pieces[0]], zr.at[0])
+    mt = gath[:, pl.ds(MW, META)]
     ei = iota((SLOTS, META), 0)
     ej = iota((SLOTS, META), 1)
     same = ((ei // 16) == ((ej % 32) // 2)) & ((ei % 2) == (ej % 2))
@@ -145,52 +239,45 @@
     et_gate = jnp.where(same & ((ej // 32 == 1) | (ej // 32 == 2)), 1.0, 0.0).astype(BF)
     t2 = lax.dot_general(et_slot, mt, NT, preferred_element_type=F32)
     samez = ((ei // 2) % 8) == (ej // 16)
-    own = pl.ds(pl.multiple_of(e * 16, 16), 16)
-
-    def dispatch(q, _):
-        sel = jnp.where(samez & ((ej // 4) % 4 == q), t2, 0.0).astype(BF)
-        sbuf[q] = jnp.dot(sel, gath[:, pl.ds(0, DW)], preferred_element_type=F32).astype(BF)
+
+    selects = [jnp.where(samez & ((ej // 4) % 4 == q), t2, 0.0).astype(BF) for q in range(4)]
+
+    def dispatch(c):
+        if c == 2:
+            wait_bytes(gath.at[pl.ds(0, 112), pieces[1]], zr.at[1])
+        cols = gath[:, pl.ds((c // 2) * (MW + META), MW)]
+        for j in range(2):
+            sbuf[c, :, pl.ds(j * MW, MW)] = jnp.dot(
+                selects[(c % 2) * 2 + j], cols, preferred_element_type=F32).astype(BF)
         for p in plane_ids:
             pltpu.make_async_remote_copy(
-                sbuf.at[q, pl.ds(pl.multiple_of(p * 16, 16), 16)], xbuf.at[q, own], ds_.at[q], dr.at[q],
+                sbuf.at[c, pl.ds(pl.multiple_of(p * 16, 16), 16)], xbuf.at[c, own], ds_.at[c], dr.at[c],
                 device_id=(h, s, p), device_id_type=MESH).start()
-        xbuf[q, own, :] = sbuf[q, own, :]
-        return 0
-
-    lax.fori_loop(0, DC, dispatch, 0)
-
-    loads[1].wait()
-    comp[...] = jnp.zeros_like(comp)
-
-    def compress(i, _):
-        at = pl.ds(pl.multiple_of(i * 1024, 1024), 1024)
-        comp[...] += lax.dot_general(xp[:, at], wk[:, at], NT, preferred_element_type=F32)
-        return 0
-
-    lax.fori_loop(0, D // 1024, compress, 0)
-    length = plen[g * NE + e]
-
-    def prompt_latents(i, _):
-        at = pl.ds(pl.multiple_of(i * 64, 64), 64)
-        rid = iota((64, 1), 0) + i * 64
-        lat, rot = latents(comp[at, :], rid.astype(F32), kg[...], freq[...])
-        pbuf[at, pl.ds(0, LAT)] = jnp.where(rid < length, lat, 0.0).astype(BF)
-        pbuf[at, pl.ds(LAT, 64)] = jnp.where(rid < length, rot, 0.0).astype(BF)
-        return 0
-
-    lax.fori_loop(0, ROWS // 64, prompt_latents, 0)
-    mine = pl.ds(pl.multiple_of(g * 16, 16), 16)
-    for hp, sp in col_ids:
-        pltpu.make_async_remote_copy(
-            pbuf.at[pl.ds(pl.multiple_of((hp * NS + sp) * 16, 16), 16)], abuf.at[mine], p1s, p1r,
-            device_id=(hp, sp, e), device_id_type=MESH).start()
-    abuf[mine, :] = pbuf[mine, :]
-
+        xbuf[c, own, :] = sbuf[c, own, :]
+
+    dispatch(0)
+    dispatch(1)
+    gather_step(1)
+    dispatch(2)
+    dispatch(3)
+    gather_step(2)
+
+    cg = lax.dot_general(mt, et_gate, NT, preferred_element_type=F32)
+    ci = iota((META, SLOTS), 0)
+    cj = iota((META, SLOTS), 1)
+    cz = (ci // 16) == ((cj // 2) % 8)
+    for q in range(4):
+        w = jnp.where(cz & ((ci // 4) % 4 == q), cg, 0.0)
+        hi = w.astype(BF)
+        wts[q] = hi
+        wts[q + 4] = (w - hi.astype(F32)).astype(BF)
     rid = iota((16, 1), 0)
     dpos = jnp.where(rid < 2, ctx[0, 0], ctx[0, 1]) + rid % 2
     lat, rot = latents(comp[pl.ds(ROWS, 16), :], dpos.astype(F32), kg[...], freq[...])
     newlat_out[:, pl.ds(0, LAT)] = lat[:DROWS].astype(BF)
     newlat_out[:, pl.ds(LAT, 64)] = rot[:DROWS].astype(BF)
+
+    gather_step(3)
 
     lane = iota((1, ROWS), 1)
     to = jnp.zeros((1, ROWS), jnp.int32)
@@ -199,6 +286,26 @@
     pi = iota((ROWS, ROWS), 0)
     pj = iota((ROWS, ROWS), 1)
     perm = jnp.where((pi // 16 == to) & (pi % 16 == pj % 16), 1.0, 0.0).astype(BF)
+    loads[2].wait()
+    loads[3].wait()
+    hacc[...] = jnp.zeros_like(hacc)
+
+    def up(q, _):
+        wait_bytes(xbuf.at[q, pl.ds(0, 240)], dr.at[q])
+        at = pl.ds(pl.multiple_of(q * DW, DW), DW)
+        hacc[...] += lax.dot_general(xbuf[q], wgu[:, at], NT, preferred_element_type=F32)
+        return 0
+
+    lax.fori_loop(0, DC - 1, up, 0)
+    gather_end()
+    order = jnp.where(
+        ((ui // 16) == ((uj % 32) // 2)) & (((ui // 2) % 8) == uj // 32) & ((ui % 2) == (uj % 2)), 1.0, 0.0).astype(BF)
+    back = jnp.where(
+        ((uj // 16) == ((ui % 32) // 2)) & (((uj // 2) % 8) == ui // 32) & ((uj % 2) == (ui % 2)), 1.0, 0.0).astype(BF)
+    hp_ = lax.dot_general(pxb[...].reshape(SLOTS, CP), wgu[:, pl.ds(CZ, CP)], NT, preferred_element_type=F32)
+    hp_hi = hp_.astype(BF)
+    hp_lo = (hp_ - hp_hi.astype(F32)).astype(BF)
+    hacc[...] += jnp.dot(order, hp_hi, preferred_element_type=F32) + jnp.dot(order, hp_lo, preferred_element_type=F32)
     wait_bytes(abuf.at[pl.ds(0, 240)], p1r)
     bbuf[...] = jnp.dot(perm, abuf[...], preferred_element_type=F32).astype(BF)
     for hp, sp in col_ids:
@@ -207,17 +314,7 @@
             device_id=(hp, sp, e), device_id_type=MESH).start()
     cbuf[mine, :] = bbuf[mine, :]
 
-    loads[2].wait()
-    loads[3].wait()
-    hacc[...] = jnp.zeros_like(hacc)
-
-    def up(q, _):
-        wait_bytes(xbuf.at[q, pl.ds(0, 240)], dr.at[q])
-        at = pl.ds(pl.multiple_of(q * DW, DW), DW)
-        hacc[...] += lax.dot_general(xbuf[q], wgu[:, at], NT, preferred_element_type=F32)
-        return 0
-
-    lax.fori_loop(0, DC, up, 0)
+    up(DC - 1, 0)
     gate = hacc[:, pl.ds(0, FB)]
     actb[...] = (gate * jax.nn.sigmoid(gate) * hacc[:, pl.ds(FB, FB)]).astype(BF)
     loads[4].wait()
@@ -232,26 +329,48 @@
         rbuf[k, own, :] = ybuf[k, own, :]
         return 0
 
-    lax.fori_loop(0, RC, down, 0)
-
-    wait_bytes(cbuf.at[pl.ds(0, 240)], p2r)
-    cache_out[...] = cbuf[...].astype(F32).T.astype(BF)
-
-    cg = lax.dot_general(gath[:, pl.ds(DW, META)], et_gate, NT, preferred_element_type=F32)
-    ci = iota((META, SLOTS), 0)
-    cj = iota((META, SLOTS), 1)
-    cz = (ci // 16) == ((cj // 2) % 8)
+    down(0, 0)
+
+    actp = jnp.dot(back, actb[...], preferred_element_type=F32).astype(BF)
+    ypb[...] = jnp.dot(actp, wd[:, pl.ds(CZ, CP)], preferred_element_type=F32).astype(BF).reshape(NS, 32, CP)
+    got = (gotr, gotl)
+    summed = (sumr, suml)
+
+    def sum_send(d, t, u):
+        dest = (s + 4 - t) % NS if d == 0 else (s + 4 + t) % NS
+        at = halves[u]
+        if t == (0 if u == d else 1):
+            src = ypb.at[dest, :, at]
+        else:
+            wait_bytes(got[d].at[t - 1, :, at], ur.at[d, t - 1, u])
+            summed[d][t - 1, :, at] = (ypb[dest, :, at].astype(F32) + got[d][t - 1, :, at].astype(F32)).astype(BF)
+            src = summed[d].at[t - 1, :, at]
+        pltpu.make_async_remote_copy(
+            src, got[d].at[t, :, at], us.at[d, t, u], ur.at[d, t, u],
+            device_id=(h, sides[d], e), device_id_type=MESH).start()
+
+    for d in range(2):
+        sum_send(d, 0, d)
+    for d in range(2):
+        sum_send(d, 1, 1 - d)
+    for k in range(1, RC):
+        down(k, 0)
+
+    def sum_step(t):
+        for d in range(2):
+            sum_send(d, t, d)
+        if t < 3:
+            for d in range(2):
+                sum_send(d, t + 1, 1 - d)
+
 
     def combine(k, _):
         wait_bytes(rbuf.at[k, pl.ds(0, 240)], rr.at[k])
         total = jnp.zeros((META, RQ), F32)
         for q in range(4):
-            w = jnp.where(cz & ((ci // 4) % 4 == q), cg, 0.0)
-            hi = w.astype(BF)
-            lo = (w - hi.astype(F32)).astype(BF)
             part = rbuf[k, :, pl.ds(q * RQ, RQ)]
-            total += jnp.dot(hi, part, preferred_element_type=F32)
-            total += jnp.dot(lo, part, preferred_element_type=F32)
+            total += jnp.dot(wts[q], part, preferred_element_type=F32)
+            total += jnp.dot(wts[q + 4], part, preferred_element_type=F32)
         fbuf[k] = total.astype(BF)
         for p in z_ids:
             pltpu.make_async_remote_copy(
@@ -260,7 +379,38 @@
         qbuf[k, my_rows, :] = fbuf[k, my_rows, :]
         return 0
 
-    lax.fori_loop(0, RC, combine, 0)
+    sum_step(1)
+    sum_step(2)
+    for k in range(RC - 2):
+        combine(k, 0)
+    sum_step(3)
+    for k in range(RC - 2, RC):
+        combine(k, 0)
+    for d in range(2):
+        for u in range(2):
+            wait_bytes(got[d].at[3, :, halves[u]], ur.at[d, 3, u])
+    done = (ypb[s].astype(F32) + gotr[3].astype(F32) + gotl[3].astype(F32)).astype(BF)
+    stacked = jnp.concatenate([done[:, q * PW:(q + 1) * PW] for q in range(PQ)], axis=0)
+    refold = jnp.where(ui == ((uj % 32) // 2) * 16 + (uj % 2) * 8 + uj // 32, 1.0, 0.0).astype(BF)
+    pfold[...] = jnp.dot(refold, stacked, preferred_element_type=F32).astype(BF)
+    for p in plane_ids:
+        pltpu.make_async_remote_copy(
+            pfold.at[pl.ds(pl.multiple_of(p * 16, 16), 16)], pback.at[own], bs, br,
+            device_id=(h, s, p), device_id_type=MESH).start()
+    pback[own, :] = pfold[own, :]
+    wait_bytes(cbuf.at[pl.ds(0, 240)], p2r)
+    cache_out[...] = cbuf[...].astype(F32).T.astype(BF)
+
+
+    fold_gate = jnp.where(fsame & ((fj // 32 == 1) | (fj // 32 == 2)), 1.0, 0.0).astype(BF)
+    cp = lax.dot_general(mtp[...], fold_gate, NT, preferred_element_type=F32)
+    cp = jnp.where(iota((4 * PQ, SLOTS), 1) % PQ == iota((4 * PQ, SLOTS), 0) // 4, cp, 0.0)
+    cp_hi = cp.astype(BF)
+    cp_lo = (cp - cp_hi.astype(F32)).astype(BF)
+    wait_bytes(pback.at[pl.ds(0, 240)], br)
+    ptot = jnp.dot(cp_hi, pback[...], preferred_element_type=F32) + jnp.dot(cp_lo, pback[...], preferred_element_type=F32)
+    for q in range(PQ):
+        moe_out[:, pl.ds(CZ + q * PW, PW)] = ptot[q * 4:q * 4 + 4, :].astype(BF)
 
     for k in range(RC):
         wait_bytes(qbuf.at[k, pl.ds(0, 112)], fr.at[k])
@@ -275,9 +425,25 @@
         wait_bytes(ybuf.at[k, pl.ds(0, 240)], rs.at[k])
     for q in range(DC):
         wait_bytes(sbuf.at[q, pl.ds(0, 240)], ds_.at[q])
-    wait_bytes(gath.at[pl.ds(0, 112)], zs)
+    for i, cols in enumerate(pieces):
+        wait_bytes(gath.at[pl.ds(0, 112), cols], zs.at[i])
+    wait_bytes(parr.at[pl.ds(0, 240)], ps)
+    wait_bytes(pback.at[pl.ds(0, 240)], bs)
+    for d in range(2):
+        for u in range(2):
+            for t in range(4):
+                if u == d or t < 3:
+                    wait_bytes(pxb.at[0, :, halves[u]], gs.at[d, t, u])
+                if u == d or t > 0:
+                    wait_bytes(ypb.at[0, :, halves[u]], us.at[d, t, u])
     wait_bytes(pbuf.at[pl.ds(0, 240)], p1s)
     wait_bytes(bbuf.at[pl.ds(0, 240)], p2s)
+
+
+def finish(a, b, c, oa, ob, oc):
+    oa[...] = a[...]
+    ob[...] = b[...]
+    oc[...] = c[...]
 
 
 def shards(
@@ -306,8 +472,8 @@
             pltpu.VMEM((FB, D), BF),
             pltpu.VMEM((ROWS + 16, D), BF),
             pltpu.VMEM((ROWS + 16, LATW), F32),
-            pltpu.VMEM((16, DW + META), BF),
-            pltpu.VMEM((NS * 16, DW + META), BF),
+            pltpu.VMEM((16, 2 * MW + META), BF),
+            pltpu.VMEM((NS * 16, 2 * MW + META), BF),
             pltpu.VMEM((DC, SLOTS, DW), BF),
             pltpu.VMEM((DC, SLOTS, DW), BF),
             pltpu.VMEM((SLOTS, 2 * FB), F32),
@@ -320,7 +486,20 @@
             pltpu.VMEM((ROWS, LATW), BF),
             pltpu.VMEM((ROWS, LATW), BF),
             pltpu.VMEM((ROWS, LATW), BF),
-            dma((5,)), dma, dma, dma((DC,)), dma((DC,)), dma, dma, dma, dma, dma((RC,)), dma((RC,)), dma((RC,)), dma((RC,)),
+            pltpu.VMEM((4 * PQ, META), BF),
+            pltpu.VMEM((SLOTS, PW), BF),
+            pltpu.VMEM((SLOTS, PW), BF),
+            pltpu.VMEM((NS, 32, CP), BF),
+            pltpu.VMEM((NS, 32, CP), BF),
+            pltpu.VMEM((3, 32, CP), BF),
+            pltpu.VMEM((3, 32, CP), BF),
+            pltpu.VMEM((4, 32, CP), BF),
+            pltpu.VMEM((4, 32, CP), BF),
+            pltpu.VMEM((SLOTS, PW), BF),
+            pltpu.VMEM((SLOTS, PW), BF),
+            pltpu.VMEM((8, META, SLOTS), BF),
+            dma((5,)), dma((2,)), dma((2,)), dma((DC,)), dma((DC,)), dma, dma, dma, dma, dma((RC,)), dma((RC,)), dma((RC,)), dma((RC,)),
+            dma, dma, dma((2, 4, 2)), dma((2, 4, 2)), dma((2, 4, 2)), dma((2, 4, 2)), dma, dma,
         ],
         compiler_params=pltpu.CompilerParams(collective_id=0, has_side_effects=True, vmem_limit_bytes=56 * 2**20),
         cost_estimate=pl.CostEstimate(flops=4 * 10**9, bytes_accessed=16 * 10**6, transcendentals=10**5),
@@ -331,6 +510,13 @@
         context_lengths.reshape(1, 2),
         prompt_hidden.reshape(ROWS, D), w_dkv.T, w_gate[0].T, w_up[0].T, w_down[0],
     )
+    moe, newlat, cache = pl.pallas_call(
+        finish,
+        out_shape=tuple(jax.ShapeDtypeStruct(v.shape, v.dtype) for v in (moe, newlat, cache)),
+        in_specs=[vm] * 3,
+        out_specs=(vm,) * 3,
+        name="results",
+    )(moe, newlat, cache)
     return (
         moe.reshape(1, 1, 1, DROWS, D),
         newlat.reshape(1, 1, 1, DROWS, LATW),

time: 95.7 us -> 71 us (0.74)
  Pallas kernels: 90.3 us -> 70.2 us
  local copies, waits for them, and re-layouts: 4.39 us -> 0 us
    pallas_call x1, Pallas kernels: 90.3 us -> 68.4 us  [shards(): pl.pallas_call(kernel, out_shape=(jax.ShapeDtypeStruct((DROWS, D), BF), j...]
    unnamed x3 -> x0, local copies, waits for them, and re-layouts: 4.39 us -> none
    pallas_call x0 -> x1, Pallas kernels: none -> 1.74 us  [shards(): pl.pallas_call(finish, out_shape=tuple((jax.ShapeDtypeStruct(v.shape, v.d...]
where the time goes in v2:
time: 71 us; the launch traced here: 70.8 us
  Pallas kernels  70.2 us (99%)
    pallas_call x1, Pallas kernels, shards(): pl.pallas_call(kernel, out_shape=(jax.ShapeDtypeStruct((DROWS, D), BF), j...  68.4 us
    pallas_call x1, Pallas kernels, shards(): pl.pallas_call(finish, out_shape=tuple((jax.ShapeDtypeStruct(v.shape, v.d...  1.74 us

profile of v2, /device:TPU:32, one launch (start us, length us, event | category | flops | bytes accessed | tf_op | source)
XLA Modules:
  0.0 70.8 jit_solution(839173083564103958)
XLA Ops:
  0.6 68.4 %layer_slice.1 = (bf16[4,5120]{1,0:T(4,128)(2,1)}, bf16[4,576]{1,0:T(4,128)(2,1)}, bf16[576,256]{1,0:T(8,128)(2,1)}) custom-call(bf16[4,5120]{1,0:T(4,128)(2,1)} %bitcast.26, f32[1,5120]{1,0:T(1,128)} %bitcast.28, f32[1,512]{1,0:T(1,128)} %bitcast.30, f32[1,64]{1,0:T(1,128)} %constant.2.clone.freq, s32[4,6]{1,0:T(4,128)} %bitcast.31, f32[4,6]{1,0:T(4,128)} %bitcast.32, ...), custom_call_target="tpu_custom_call" | custom-call | flops 4000000000 | bytes 16000000 | tf_op jit(solution)/shard_map/layer_slice/pallas_call | solution.py:459
  69.1 1.7 %results.1 = (bf16[4,5120]{1,0:T(4,128)(2,1)}, bf16[4,576]{1,0:T(4,128)(2,1)}, bf16[576,256]{1,0:T(8,128)(2,1)}) custom-call(bf16[4,5120]{1,0:T(4,128)(2,1)} %get-tuple-element.9.a, bf16[4,576]{1,0:T(4,128)(2,1)} %get-tuple-element.10.b, bf16[576,256]{1,0:T(8,128)(2,1)} %get-tuple-element.11.c), custom_call_target="tpu_custom_call" | custom-call | tf_op jit(solution)/shard_map/results/pallas_call | solution.py:513

commit v3 on v2

--- a/solution.py
+++ b/solution.py
@@ -26,22 +26,21 @@
 CZ = 3072
 CP = D - CZ
 HP = CP // 2
-DC = 4
-DW = CZ // DC
-MW = CZ // 8
+MW = (128, 128, 256, 256)
+DC = len(MW)
+AT = tuple(4 * sum(MW[:i]) for i in range(DC))
 META = 128
+PIECE = tuple(pl.ds(META * (i > 0) + sum(MW[:i]), MW[i] + META * (i == 0)) for i in range(DC))
+GROUP = tuple(pl.ds(META + sum(MW[:i]), MW[i]) for i in range(DC))
 RC = 3
 RW = CZ // RC
 RQ = RW // 4
 PQ = 8
 PW = CP // PQ
 
-PLANE = (
-    (0, 1), (1, 0), (0, 3), (3, 0), (1, 1), (3, 3), (1, 3), (3, 1),
-    (0, 2), (2, 0), (1, 2), (2, 1), (3, 2), (2, 3), (2, 2),
-)
+PLANE = ((2, 2), (0, 1), (0, 3), (2, 1), (2, 3), (1, 0), (3, 0), (1, 2), (3, 2), (1, 1), (3, 3), (1, 3), (3, 1), (0, 2), (2, 0))
 ZOFF = (4, 3, 5, 2, 6, 1, 7)
-COL = ((1, 0), (0, 1), (0, 7), (1, 1), (1, 7), (0, 2), (0, 6), (1, 2), (1, 6), (0, 3), (0, 5), (1, 3), (1, 5), (0, 4), (1, 4))
+COL = ((0, 4), (1, 4), (0, 3), (0, 5), (1, 3), (1, 5), (0, 2), (0, 6), (1, 2), (1, 6), (0, 1), (0, 7), (1, 1), (1, 7), (1, 0))
 
 NT = (((1,), (1,)), ((), ()))
 
@@ -68,12 +67,13 @@
 
 
 def kernel(
-    dh, ng, kg, freq, ids, gates, owner, plen, ctx, ph_hbm, wk_hbm, wg_hbm, wu_hbm, wd_hbm,
+    dh_hbm, ng_hbm, kg_hbm, freq_hbm, ids_hbm, gates_hbm, owner_hbm, plen_hbm, ctx_hbm, ph_hbm, wk_hbm, wg_hbm, wu_hbm, wd_hbm,
     moe_out, newlat_out, cache_out,
     ph, wk, wgu, wd, xp, comp, msg, gath, sbuf, xbuf, hacc, actb, ybuf, rbuf, fbuf, qbuf, pbuf, abuf, bbuf, cbuf,
     mtp, pmsg, parr, pxb, ypb, sumr, suml, gotr, gotl, pfold, pback, wts,
+    dh, ng, kg, freq, ids, gates, owner, plen, ctx,
     lsem, zs, zr, ds_, dr, p1s, p1r, p2s, p2r, rs, rr, fs, fr,
-    ps, pr, gs, gr, us, ur, bs, br,
+    ps, pr, gs, gr, us, ur, bs, br, isem,
 ):
     h = lax.axis_index("half")
     s = lax.axis_index("seq")
@@ -86,11 +86,18 @@
     col_ids = [((h + dh_) % 2, (s + d) % NS) for dh_, d in COL]
 
     barrier = pltpu.get_barrier_semaphore()
+    for hp, sp in col_ids:
+        pl.semaphore_signal(barrier, inc=1, device_id=(hp, sp, e), device_id_type=MESH)
     for p in plane_ids:
         pl.semaphore_signal(barrier, inc=1, device_id=(h, s, p), device_id_type=MESH)
-    for hp, sp in col_ids:
-        pl.semaphore_signal(barrier, inc=1, device_id=(hp, sp, e), device_id_type=MESH)
-
+
+    small = [
+        pltpu.make_async_copy(src, dst, isem.at[i]) for i, (src, dst) in enumerate((
+            (dh_hbm, dh), (ng_hbm, ng), (ids_hbm, ids), (gates_hbm, gates), (kg_hbm, kg), (freq_hbm, freq),
+            (owner_hbm, owner), (plen_hbm, plen), (ctx_hbm, ctx)))
+    ]
+    for c in small:
+        c.start()
     loads = [
         pltpu.make_async_copy(ph_hbm, ph, lsem.at[0]),
         pltpu.make_async_copy(wk_hbm, wk, lsem.at[1]),
@@ -101,12 +108,14 @@
     for c in loads:
         c.start()
 
+    for c in small:
+        c.wait()
+
     dec = dh[...].astype(F32)
     ms = jnp.mean(dec * dec, axis=-1, keepdims=True)
     dn = dec * lax.rsqrt(ms + 1e-06) * ng[...]
-    for i, at in enumerate((0, MW + META)):
-        msg[:, pl.ds(at, MW)] = jnp.concatenate(
-            [dn[:, (4 * i + q) * MW:(4 * i + q + 1) * MW] for q in range(4)], axis=0).astype(BF)
+    for at, w, cols in zip(AT, MW, GROUP):
+        msg[:, cols] = jnp.concatenate([dn[:, at + q * w:at + (q + 1) * w] for q in range(4)], axis=0).astype(BF)
     xp[pl.ds(ROWS, 16), :] = jnp.concatenate([dn, jnp.zeros((12, D), F32)], axis=0).astype(BF)
     lane = iota((1, META), 1)
     kind = lane // 32
@@ -126,7 +135,7 @@
         rows.append(jnp.where((named > 0) & (before == cl), val, 0.0))
         before = before + named
     meta4 = jnp.concatenate(rows, axis=0)
-    msg[:, pl.ds(MW, META)] = jnp.concatenate([meta4] * 4, axis=0).astype(BF)
+    msg[:, pl.ds(0, META)] = jnp.concatenate([meta4] * 4, axis=0).astype(BF)
 
     mtp[...] = jnp.concatenate([meta4] * PQ, axis=0).astype(BF)
     fi = iota((SLOTS, META), 0)
@@ -138,12 +147,22 @@
     dcols = jnp.concatenate([dn[:, CZ + q * PW:CZ + (q + 1) * PW] for q in range(PQ)], axis=0).astype(BF)
     pmsg[...] = jnp.dot(self_, dcols, preferred_element_type=F32).astype(BF)
 
+    loads[0].wait()
+
+    def pnorm(i, _):
+        at = pl.ds(pl.multiple_of(i * 32, 32), 32)
+        v = ph[at, :].astype(F32)
+        m = jnp.mean(v * v, axis=-1, keepdims=True)
+        xp[at, :] = (v * lax.rsqrt(m + 1e-06) * ng[...]).astype(BF)
+        return 0
+
+    lax.fori_loop(0, ROWS // 32, pnorm, 0)
+
     pl.semaphore_wait(barrier, len(PLANE) + len(COL))
 
     my_rows = pl.ds(pl.multiple_of(s * 16, 16), 16)
     own = pl.ds(pl.multiple_of(e * 16, 16), 16)
-    pieces = (pl.ds(0, MW + META), pl.ds(MW + META, MW))
-    for i, cols in enumerate(pieces):
+    for i, cols in enumerate(PIECE):
         for p in z_ids:
             pltpu.make_async_remote_copy(
                 msg.at[:, cols], gath.at[my_rows, cols], zs.at[i], zr.at[i], device_id=(h, p, e), device_id_type=MESH).start()
@@ -154,17 +173,6 @@
     gath[my_rows, :] = msg[...]
     parr[own, :] = pmsg[own, :]
 
-    loads[0].wait()
-
-    def pnorm(i, _):
-        at = pl.ds(pl.multiple_of(i * 32, 32), 32)
-        v = ph[at, :].astype(F32)
-        m = jnp.mean(v * v, axis=-1, keepdims=True)
-        xp[at, :] = (v * lax.rsqrt(m + 1e-06) * ng[...]).astype(BF)
-        return 0
-
-    lax.fori_loop(0, ROWS // 32, pnorm, 0)
-
     right = (s + 1) % NS
     left = (s + 7) % NS
 
@@ -192,6 +200,27 @@
         for d in range(2):
             wait_bytes(pxb.at[block(d, 4), :, halves[d]], gr.at[d, 3, d])
             wait_bytes(pxb.at[block(d, 3), :, halves[1 - d]], gr.at[d, 2, 1 - d])
+
+    loads[1].wait()
+    comp[...] = jnp.zeros_like(comp)
+
+    def compress(i, _):
+        at = pl.ds(pl.multiple_of(i * 1024, 1024), 1024)
+        comp[...] += lax.dot_general(xp[:, at], wk[:, at], NT, preferred_element_type=F32)
+        return 0
+
+    lax.fori_loop(0, D // 1024, compress, 0)
+    length = plen[g * NE + e]
+
+    def prompt_latents(i, _):
+        at = pl.ds(pl.multiple_of(i * 64, 64), 64)
+        rid = iota((64, 1), 0) + i * 64
+        lat, rot = latents(comp[at, :], rid.astype(F32), kg[...], freq[...])
+        pbuf[at, pl.ds(0, LAT)] = jnp.where(rid < length, lat, 0.0).astype(BF)
+        pbuf[at, pl.ds(LAT, 64)] = jnp.where(rid < length, rot, 0.0).astype(BF)
+        return 0
+
+    lax.fori_loop(0, ROWS // 64, prompt_latents, 0)
 
     ui = iota((SLOTS, SLOTS), 0)
     uj = iota((SLOTS, SLOTS), 1)
@@ -201,27 +230,6 @@
     for q in range(PQ):
         pxb[s, :, pl.ds(q * PW, PW)] = flat[q * 32:(q + 1) * 32, :]
     gather_step(0)
-
-    loads[1].wait()
-    comp[...] = jnp.zeros_like(comp)
-
-    def compress(i, _):
-        at = pl.ds(pl.multiple_of(i * 1024, 1024), 1024)
-        comp[...] += lax.dot_general(xp[:, at], wk[:, at], NT, preferred_element_type=F32)
-        return 0
-
-    lax.fori_loop(0, D // 1024, compress, 0)
-    length = plen[g * NE + e]
-
-    def prompt_latents(i, _):
-        at = pl.ds(pl.multiple_of(i * 64, 64), 64)
-        rid = iota((64, 1), 0) + i * 64
-        lat, rot = latents(comp[at, :], rid.astype(F32), kg[...], freq[...])
-        pbuf[at, pl.ds(0, LAT)] = jnp.where(rid < length, lat, 0.0).astype(BF)
-        pbuf[at, pl.ds(LAT, 64)] = jnp.where(rid < length, rot, 0.0).astype(BF)
-        return 0
-
-    lax.fori_loop(0, ROWS // 64, prompt_latents, 0)
     mine = pl.ds(pl.multiple_of(g * 16, 16), 16)
     for hp, sp in col_ids:
         pltpu.make_async_remote_copy(
@@ -230,8 +238,8 @@
     abuf[mine, :] = pbuf[mine, :]
 
 
-    wait_bytes(gath.at[pl.ds(0, 112), pieces[0]], zr.at[0])
-    mt = gath[:, pl.ds(MW, META)]
+    wait_bytes(gath.at[pl.ds(0, 112), PIECE[0]], zr.at[0])
+    mt = gath[:, pl.ds(0, META)]
     ei = iota((SLOTS, META), 0)
     ej = iota((SLOTS, META), 1)
     same = ((ei // 16) == ((ej % 32) // 2)) & ((ei % 2) == (ej % 2))
@@ -240,20 +248,19 @@
     t2 = lax.dot_general(et_slot, mt, NT, preferred_element_type=F32)
     samez = ((ei // 2) % 8) == (ej // 16)
 
-    selects = [jnp.where(samez & ((ej // 4) % 4 == q), t2, 0.0).astype(BF) for q in range(4)]
-
     def dispatch(c):
-        if c == 2:
-            wait_bytes(gath.at[pl.ds(0, 112), pieces[1]], zr.at[1])
-        cols = gath[:, pl.ds((c // 2) * (MW + META), MW)]
-        for j in range(2):
-            sbuf[c, :, pl.ds(j * MW, MW)] = jnp.dot(
-                selects[(c % 2) * 2 + j], cols, preferred_element_type=F32).astype(BF)
+        if c > 0:
+            wait_bytes(gath.at[pl.ds(0, 112), PIECE[c]], zr.at[c])
+        for q in range(4):
+            pick = jnp.where(samez & ((ej // 4) % 4 == q), t2, 0.0).astype(BF)
+            sbuf[:, pl.ds(AT[c] + q * MW[c], MW[c])] = jnp.dot(
+                pick, gath[:, GROUP[c]], preferred_element_type=F32).astype(BF)
+        cols = pl.ds(AT[c], 4 * MW[c])
         for p in plane_ids:
             pltpu.make_async_remote_copy(
-                sbuf.at[c, pl.ds(pl.multiple_of(p * 16, 16), 16)], xbuf.at[c, own], ds_.at[c], dr.at[c],
+                sbuf.at[pl.ds(pl.multiple_of(p * 16, 16), 16), cols], xbuf.at[own, cols], ds_.at[c], dr.at[c],
                 device_id=(h, s, p), device_id_type=MESH).start()
-        xbuf[c, own, :] = sbuf[c, own, :]
+        xbuf[own, cols] = sbuf[own, cols]
 
     dispatch(0)
     dispatch(1)
@@ -290,13 +297,13 @@
     loads[3].wait()
     hacc[...] = jnp.zeros_like(hacc)
 
-    def up(q, _):
-        wait_bytes(xbuf.at[q, pl.ds(0, 240)], dr.at[q])
-        at = pl.ds(pl.multiple_of(q * DW, DW), DW)
-        hacc[...] += lax.dot_general(xbuf[q], wgu[:, at], NT, preferred_element_type=F32)
-        return 0
-
-    lax.fori_loop(0, DC - 1, up, 0)
+    def up(c):
+        cols = pl.ds(AT[c], 4 * MW[c])
+        wait_bytes(xbuf.at[pl.ds(0, 240), cols], dr.at[c])
+        hacc[...] += lax.dot_general(xbuf[:, cols], wgu[:, cols], NT, preferred_element_type=F32)
+
+    for c in range(DC - 1):
+        up(c)
     gather_end()
     order = jnp.where(
         ((ui // 16) == ((uj % 32) // 2)) & (((ui // 2) % 8) == uj // 32) & ((ui % 2) == (uj % 2)), 1.0, 0.0).astype(BF)
@@ -314,7 +321,7 @@
             device_id=(hp, sp, e), device_id_type=MESH).start()
     cbuf[mine, :] = bbuf[mine, :]
 
-    up(DC - 1, 0)
+    up(DC - 1)
     gate = hacc[:, pl.ds(0, FB)]
     actb[...] = (gate * jax.nn.sigmoid(gate) * hacc[:, pl.ds(FB, FB)]).astype(BF)
     loads[4].wait()
@@ -423,9 +430,9 @@
     for k in range(RC):
         wait_bytes(fbuf.at[k, pl.ds(0, 112)], fs.at[k])
         wait_bytes(ybuf.at[k, pl.ds(0, 240)], rs.at[k])
-    for q in range(DC):
-        wait_bytes(sbuf.at[q, pl.ds(0, 240)], ds_.at[q])
-    for i, cols in enumerate(pieces):
+    for c in range(DC):
+        wait_bytes(sbuf.at[pl.ds(0, 240), pl.ds(AT[c], 4 * MW[c])], ds_.at[c])
+    for i, cols in enumerate(PIECE):
         wait_bytes(gath.at[pl.ds(0, 112), cols], zs.at[i])
     wait_bytes(parr.at[pl.ds(0, 240)], ps)
     wait_bytes(pback.at[pl.ds(0, 240)], bs)
@@ -453,7 +460,6 @@
     freq = 10000.0 ** (-(np.arange(32, dtype=np.float64) * 2.0 / 64))
     freq = jnp.asarray(np.concatenate([freq, freq])[None, :], F32)
     vm = pl.BlockSpec(memory_space=pltpu.VMEM)
-    sm = pl.BlockSpec(memory_space=pltpu.SMEM)
     hbm = pl.BlockSpec(memory_space=pl.ANY)
     dma = pltpu.SemaphoreType.DMA
     moe, newlat, cache = pl.pallas_call(
@@ -463,7 +469,7 @@
             jax.ShapeDtypeStruct((DROWS, LATW), BF),
             jax.ShapeDtypeStruct((LATW, ROWS), BF),
         ),
-        in_specs=[vm] * 4 + [sm] * 5 + [hbm] * 5,
+        in_specs=[hbm] * 14,
         out_specs=(vm, vm, vm),
         scratch_shapes=[
             pltpu.VMEM((ROWS, D), BF),
@@ -472,10 +478,10 @@
             pltpu.VMEM((FB, D), BF),
             pltpu.VMEM((ROWS + 16, D), BF),
             pltpu.VMEM((ROWS + 16, LATW), F32),
-            pltpu.VMEM((16, 2 * MW + META), BF),
-            pltpu.VMEM((NS * 16, 2 * MW + META), BF),
-            pltpu.VMEM((DC, SLOTS, DW), BF),
-            pltpu.VMEM((DC, SLOTS, DW), BF),
+            pltpu.VMEM((16, sum(MW) + META), BF),
+            pltpu.VMEM((NS * 16, sum(MW) + META), BF),
+            pltpu.VMEM((SLOTS, CZ), BF),
+            pltpu.VMEM((SLOTS, CZ), BF),
             pltpu.VMEM((SLOTS, 2 * FB), F32),
             pltpu.VMEM((SLOTS, FB), BF),
             pltpu.VMEM((RC, SLOTS, RW), BF),
@@ -498,8 +504,17 @@
             pltpu.VMEM((SLOTS, PW), BF),
             pltpu.VMEM((SLOTS, PW), BF),
             pltpu.VMEM((8, META, SLOTS), BF),
-            dma((5,)), dma((2,)), dma((2,)), dma((DC,)), dma((DC,)), dma, dma, dma, dma, dma((RC,)), dma((RC,)), dma((RC,)), dma((RC,)),
-            dma, dma, dma((2, 4, 2)), dma((2, 4, 2)), dma((2, 4, 2)), dma((2, 4, 2)), dma, dma,
+            pltpu.VMEM((DROWS, D), BF),
+            pltpu.VMEM((1, D), F32),
+            pltpu.VMEM((1, LAT), F32),
+            pltpu.VMEM((1, 64), F32),
+            pltpu.SMEM((DROWS, TOP), jnp.int32),
+            pltpu.SMEM((DROWS, TOP), F32),
+            pltpu.SMEM((NG, NE), jnp.int32),
+            pltpu.SMEM((NG * NE,), jnp.int32),
+            pltpu.SMEM((1, 2), jnp.int32),
+            dma((5,)), dma((DC,)), dma((DC,)), dma((DC,)), dma((DC,)), dma, dma, dma, dma, dma((RC,)), dma((RC,)), dma((RC,)), dma((RC,)),
+            dma, dma, dma((2, 4, 2)), dma((2, 4, 2)), dma((2, 4, 2)), dma((2, 4, 2)), dma, dma, dma((9,)),
         ],
         compiler_params=pltpu.CompilerParams(collective_id=0, has_side_effects=True, vmem_limit_bytes=56 * 2**20),
         cost_estimate=pl.CostEstimate(flops=4 * 10**9, bytes_accessed=16 * 10**6, transcendentals=10**5),

time: 71 us -> 68.3 us (0.962)
  Pallas kernels: 70.2 us -> 67.6 us
    pallas_call x1, Pallas kernels: 68.4 us -> 65.8 us  [shards(): pl.pallas_call(kernel, out_shape=(jax.ShapeDtypeStruct((DROWS, D), BF), j...]
where the time goes in v3:
time: 68.3 us; the launch traced here: 68.2 us
  Pallas kernels  67.6 us (99%)
    pallas_call x1, Pallas kernels, shards(): pl.pallas_call(kernel, out_shape=(jax.ShapeDtypeStruct((DROWS, D), BF), j...  65.8 us
    pallas_call x1, Pallas kernels, shards(): pl.pallas_call(finish, out_shape=tuple((jax.ShapeDtypeStruct(v.shape, v.d...  1.74 us

profile of v3, /device:TPU:32, one launch (start us, length us, event | category | flops | bytes accessed | tf_op | source)
XLA Modules:
  0.0 68.2 jit_solution(12063502593305129353)
XLA Ops:
  0.6 65.8 %layer_slice.1 = (bf16[4,5120]{1,0:T(4,128)(2,1)}, bf16[4,576]{1,0:T(4,128)(2,1)}, bf16[576,256]{1,0:T(8,128)(2,1)}) custom-call(bf16[4,5120]{1,0:T(4,128)(2,1)} %bitcast.26, f32[1,5120]{1,0:T(1,128)} %bitcast.28, f32[1,512]{1,0:T(1,128)} %bitcast.30, f32[1,64]{1,0:T(1,128)} %constant.2.clone.freq_hbm, s32[4,6]{1,0:T(4,128)} %bitcast.31, f32[4,6]{1,0:T(4,128)} %bitcast.32, ...), custom_call_target="tpu_custom_call" | custom-call | flops 4000000000 | bytes 16000000 | tf_op jit(solution)/shard_map/layer_slice/pallas_call | solution.py:465
  66.5 1.7 %results.1 = (bf16[4,5120]{1,0:T(4,128)(2,1)}, bf16[4,576]{1,0:T(4,128)(2,1)}, bf16[576,256]{1,0:T(8,128)(2,1)}) custom-call(bf16[4,5120]{1,0:T(4,128)(2,1)} %get-tuple-element.9.a, bf16[4,576]{1,0:T(4,128)(2,1)} %get-tuple-element.10.b, bf16[576,256]{1,0:T(8,128)(2,1)} %get-tuple-element.11.c), custom_call_target="tpu_custom_call" | custom-call | tf_op jit(solution)/shard_map/results/pallas_call | solution.py:528

commit v4 on v3

--- a/solution.py
+++ b/solution.py
@@ -162,14 +162,19 @@
 
     my_rows = pl.ds(pl.multiple_of(s * 16, 16), 16)
     own = pl.ds(pl.multiple_of(e * 16, 16), 16)
-    for i, cols in enumerate(PIECE):
+    def send_piece(i):
         for p in z_ids:
             pltpu.make_async_remote_copy(
-                msg.at[:, cols], gath.at[my_rows, cols], zs.at[i], zr.at[i], device_id=(h, p, e), device_id_type=MESH).start()
+                msg.at[:, PIECE[i]], gath.at[my_rows, PIECE[i]], zs.at[i], zr.at[i],
+                device_id=(h, p, e), device_id_type=MESH).start()
+
+    send_piece(0)
     for p in plane_ids:
         pltpu.make_async_remote_copy(
             pmsg.at[pl.ds(pl.multiple_of(p * 16, 16), 16)], parr.at[own], ps, pr,
             device_id=(h, s, p), device_id_type=MESH).start()
+    for i in range(1, DC):
+        send_piece(i)
     gath[my_rows, :] = msg[...]
     parr[own, :] = pmsg[own, :]
 
@@ -293,6 +298,14 @@
     pi = iota((ROWS, ROWS), 0)
     pj = iota((ROWS, ROWS), 1)
     perm = jnp.where((pi // 16 == to) & (pi % 16 == pj % 16), 1.0, 0.0).astype(BF)
+    wait_bytes(abuf.at[pl.ds(0, 240)], p1r)
+    bbuf[...] = jnp.dot(perm, abuf[...], preferred_element_type=F32).astype(BF)
+    for hp, sp in col_ids:
+        pltpu.make_async_remote_copy(
+            bbuf.at[pl.ds(pl.multiple_of((hp * NS + sp) * 16, 16), 16)], cbuf.at[mine], p2s, p2r,
+            device_id=(hp, sp, e), device_id_type=MESH).start()
+    cbuf[mine, :] = bbuf[mine, :]
+
     loads[2].wait()
     loads[3].wait()
     hacc[...] = jnp.zeros_like(hacc)
@@ -313,14 +326,6 @@
     hp_hi = hp_.astype(BF)
     hp_lo = (hp_ - hp_hi.astype(F32)).astype(BF)
     hacc[...] += jnp.dot(order, hp_hi, preferred_element_type=F32) + jnp.dot(order, hp_lo, preferred_element_type=F32)
-    wait_bytes(abuf.at[pl.ds(0, 240)], p1r)
-    bbuf[...] = jnp.dot(perm, abuf[...], preferred_element_type=F32).astype(BF)
-    for hp, sp in col_ids:
-        pltpu.make_async_remote_copy(
-            bbuf.at[pl.ds(pl.multiple_of((hp * NS + sp) * 16, 16), 16)], cbuf.at[mine], p2s, p2r,
-            device_id=(hp, sp, e), device_id_type=MESH).start()
-    cbuf[mine, :] = bbuf[mine, :]
-
     up(DC - 1)
     gate = hacc[:, pl.ds(0, FB)]
     actb[...] = (gate * jax.nn.sigmoid(gate) * hacc[:, pl.ds(FB, FB)]).astype(BF)
@@ -388,11 +393,10 @@
 
     sum_step(1)
     sum_step(2)
-    for k in range(RC - 2):
-        combine(k, 0)
     sum_step(3)
-    for k in range(RC - 2, RC):
-        combine(k, 0)
+    combine(0, 0)
+    combine(1, 0)
+    combine(2, 0)
     for d in range(2):
         for u in range(2):
             wait_bytes(got[d].at[3, :, halves[u]], ur.at[d, 3, u])

time: 68.3 us -> 66.5 us (0.974)
  Pallas kernels: 67.6 us -> 65.8 us
    pallas_call x1, Pallas kernels: 65.8 us -> 64 us  [shards(): pl.pallas_call(kernel, out_shape=(jax.ShapeDtypeStruct((DROWS, D), BF), j...]
where the time goes in v4:
time: 66.5 us; the launch traced here: 66.4 us
  Pallas kernels  65.8 us (99%)
    pallas_call x1, Pallas kernels, shards(): pl.pallas_call(kernel, out_shape=(jax.ShapeDtypeStruct((DROWS, D), BF), j...  64 us
    pallas_call x1, Pallas kernels, shards(): pl.pallas_call(finish, out_shape=tuple((jax.ShapeDtypeStruct(v.shape, v.d...  1.74 us

profile of v4, /device:TPU:32, one launch (start us, length us, event | category | flops | bytes accessed | tf_op | source)
XLA Modules:
  0.0 66.4 jit_solution(16513656151418767753)
XLA Ops:
  0.6 64.0 %layer_slice.1 = (bf16[4,5120]{1,0:T(4,128)(2,1)}, bf16[4,576]{1,0:T(4,128)(2,1)}, bf16[576,256]{1,0:T(8,128)(2,1)}) custom-call(bf16[4,5120]{1,0:T(4,128)(2,1)} %bitcast.26, f32[1,5120]{1,0:T(1,128)} %bitcast.28, f32[1,512]{1,0:T(1,128)} %bitcast.30, f32[1,64]{1,0:T(1,128)} %constant.2.clone.freq_hbm, s32[4,6]{1,0:T(4,128)} %bitcast.31, f32[4,6]{1,0:T(4,128)} %bitcast.32, ...), custom_call_target="tpu_custom_call" | custom-call | flops 4000000000 | bytes 16000000 | tf_op jit(solution)/shard_map/layer_slice/pallas_call | solution.py:469
  64.7 1.7 %results.1 = (bf16[4,5120]{1,0:T(4,128)(2,1)}, bf16[4,576]{1,0:T(4,128)(2,1)}, bf16[576,256]{1,0:T(8,128)(2,1)}) custom-call(bf16[4,5120]{1,0:T(4,128)(2,1)} %get-tuple-element.9.a, bf16[4,576]{1,0:T(4,128)(2,1)} %get-tuple-element.10.b, bf16[576,256]{1,0:T(8,128)(2,1)} %get-tuple-element.11.c), custom_call_target="tpu_custom_call" | custom-call | tf_op jit(solution)/shard_map/results/pallas_call | solution.py:532

commit v5 on v4

--- a/solution.py
+++ b/solution.py
@@ -274,6 +274,23 @@
     dispatch(3)
     gather_step(2)
 
+    gather_step(3)
+
+    lane = iota((1, ROWS), 1)
+    to = jnp.zeros((1, ROWS), jnp.int32)
+    for k in range(NG):
+        to = to + jnp.where(lane // 16 == k, owner[e, k], 0)
+    pi = iota((ROWS, ROWS), 0)
+    pj = iota((ROWS, ROWS), 1)
+    perm = jnp.where((pi // 16 == to) & (pi % 16 == pj % 16), 1.0, 0.0).astype(BF)
+    wait_bytes(abuf.at[pl.ds(0, 240)], p1r)
+    bbuf[...] = jnp.dot(perm, abuf[...], preferred_element_type=F32).astype(BF)
+    for hp, sp in col_ids:
+        pltpu.make_async_remote_copy(
+            bbuf.at[pl.ds(pl.multiple_of((hp * NS + sp) * 16, 16), 16)], cbuf.at[mine], p2s, p2r,
+            device_id=(hp, sp, e), device_id_type=MESH).start()
+    cbuf[mine, :] = bbuf[mine, :]
+
     cg = lax.dot_general(mt, et_gate, NT, preferred_element_type=F32)
     ci = iota((META, SLOTS), 0)
     cj = iota((META, SLOTS), 1)
@@ -288,23 +305,6 @@
     lat, rot = latents(comp[pl.ds(ROWS, 16), :], dpos.astype(F32), kg[...], freq[...])
     newlat_out[:, pl.ds(0, LAT)] = lat[:DROWS].astype(BF)
     newlat_out[:, pl.ds(LAT, 64)] = rot[:DROWS].astype(BF)
-
-    gather_step(3)
-
-    lane = iota((1, ROWS), 1)
-    to = jnp.zeros((1, ROWS), jnp.int32)
-    for k in range(NG):
-        to = to + jnp.where(lane // 16 == k, owner[e, k], 0)
-    pi = iota((ROWS, ROWS), 0)
-    pj = iota((ROWS, ROWS), 1)
-    perm = jnp.where((pi // 16 == to) & (pi % 16 == pj % 16), 1.0, 0.0).astype(BF)
-    wait_bytes(abuf.at[pl.ds(0, 240)], p1r)
-    bbuf[...] = jnp.dot(perm, abuf[...], preferred_element_type=F32).astype(BF)
-    for hp, sp in col_ids:
-        pltpu.make_async_remote_copy(
-            bbuf.at[pl.ds(pl.multiple_of((hp * NS + sp) * 16, 16), 16)], cbuf.at[mine], p2s, p2r,
-            device_id=(hp, sp, e), device_id_type=MESH).start()
-    cbuf[mine, :] = bbuf[mine, :]
 
     loads[2].wait()
     loads[3].wait()

time: 66.5 us -> 67 us (level)
  no operation moved by 1% of the time
where the time goes in v5:
time: 67 us; the launch traced here: 66.9 us
  Pallas kernels  66.3 us (99%)
    pallas_call x1, Pallas kernels, shards(): pl.pallas_call(kernel, out_shape=(jax.ShapeDtypeStruct((DROWS, D), BF), j...  64.5 us
    pallas_call x1, Pallas kernels, shards(): pl.pallas_call(finish, out_shape=tuple((jax.ShapeDtypeStruct(v.shape, v.d...  1.74 us

profile of v5, /device:TPU:32, one launch (start us, length us, event | category | flops | bytes accessed | tf_op | source)
XLA Modules:
  0.0 66.9 jit_solution(12261517560969901842)
XLA Ops:
  0.6 64.5 %layer_slice.1 = (bf16[4,5120]{1,0:T(4,128)(2,1)}, bf16[4,576]{1,0:T(4,128)(2,1)}, bf16[576,256]{1,0:T(8,128)(2,1)}) custom-call(bf16[4,5120]{1,0:T(4,128)(2,1)} %bitcast.26, f32[1,5120]{1,0:T(1,128)} %bitcast.28, f32[1,512]{1,0:T(1,128)} %bitcast.30, f32[1,64]{1,0:T(1,128)} %constant.2.clone.freq_hbm, s32[4,6]{1,0:T(4,128)} %bitcast.31, f32[4,6]{1,0:T(4,128)} %bitcast.32, ...), custom_call_target="tpu_custom_call" | custom-call | flops 4000000000 | bytes 16000000 | tf_op jit(solution)/shard_map/layer_slice/pallas_call | solution.py:469
  65.2 1.7 %results.1 = (bf16[4,5120]{1,0:T(4,128)(2,1)}, bf16[4,576]{1,0:T(4,128)(2,1)}, bf16[576,256]{1,0:T(8,128)(2,1)}) custom-call(bf16[4,5120]{1,0:T(4,128)(2,1)} %get-tuple-element.9.a, bf16[4,576]{1,0:T(4,128)(2,1)} %get-tuple-element.10.b, bf16[576,256]{1,0:T(8,128)(2,1)} %get-tuple-element.11.c), custom_call_target="tpu_custom_call" | custom-call | tf_op jit(solution)/shard_map/results/pallas_call | solution.py:532
